TPU v7x, 32 devices: a whole 2x2x4 slice. The times are simulated.
32 devices in a mesh: tensor: 8 (over y, x, core), dp: 4 (over z).
Axes of the slice: x: 2, y: 2, z: 4, core: 2. Of those that a mesh axis runs over, the one named last changes fastest.
Arguments:
- tokens: bfloat16 [6144, 6144], P('dp', 'tensor'), may hold values from -9 to 9
- expert_ids: int32 [6144, 2], P('dp'), may hold values from 0 to 7, as said below
- gate_probs: float32 [6144, 2], P('dp'), may hold values from 0.2 to 1
- gate_weight: bfloat16 [6144, 8192], P(None, 'tensor'), may hold values from -0.078125 to 0.078125
- up_weight: bfloat16 [6144, 8192], P(None, 'tensor'), may hold values from -0.078125 to 0.078125
- down_weight: bfloat16 [8192, 6144], P('tensor'), may hold values from -0.09375 to 0.09375
Outputs:
- expert_out: bfloat16 [6144, 6144], P('dp', 'tensor')
- peaks: float32 [2], replicated
Inputs may be any that keep to these rules, and one draw needn't show every extreme that they name: `expert_ids`: each row names two different experts. In each aligned block of 1536 rows at most 768 rows name expert 0, and in some block exactly 768 do.
All inputs are finite; a program needn't handle non-finite values.
Results may differ from a plain program's by a relative error of at most 0.02.
Values may be sent and summed in bfloat16 or wider, within the bound.
No kernel may reach another device: no remote copies, remote signals or barrier semaphores. Data moves between devices by JAX's collectives and lax.ppermute only.
A program may use at most 128 MiB of HBM per device.

v0:
```python
import math

import jax
import jax.numpy as jnp
from jax import lax
from jax.experimental import pallas as pl
from jax.experimental.pallas import tpu as pltpu
from jax.sharding import PartitionSpec as P

CAP = 768
CLIP_SHARE = 0.25
LANES = 128
ROW_CHUNKS = 2
BF16 = jnp.bfloat16
F32 = jnp.float32
MIB = 1 << 20
EXPAND_MIB = 24
AHEAD = 3


def params(mib):
    return pltpu.CompilerParams(vmem_limit_bytes=mib * MIB)


TINY = pl.CostEstimate(flops=1, bytes_accessed=1, transcendentals=0)


def across(block, bit):
    count = lax.axis_size("tensor")
    return lax.ppermute(block, "tensor", [(r, r ^ 1 << bit) for r in range(count)])


def iota(shape, dim):
    return lax.broadcasted_iota(jnp.int32, shape, dim)


def slots_of(ids_ref):
    tokens = ids_ref.shape[1]
    rows = tokens // LANES
    padded = (rows + 15) // 16 * 16
    hit = jnp.where((ids_ref[0:1, :] == 0) | (ids_ref[1:2, :] == 0), 1.0, 0.0)
    grid = jnp.concatenate(
        [hit[:, LANES * k : LANES * (k + 1)] for k in range(rows)]
        + [jnp.zeros((padded - rows, LANES), F32)],
        axis=0,
    )
    flat = grid.astype(BF16)
    upto = (iota((LANES, LANES), 0) <= iota((LANES, LANES), 1)).astype(F32).astype(BF16)
    before = (iota((padded, padded), 1) < iota((padded, padded), 0)).astype(F32).astype(BF16)
    within = jnp.dot(flat, upto, preferred_element_type=F32)
    offset = jnp.sum(jnp.dot(before, flat, preferred_element_type=F32), axis=1, keepdims=True)
    return jnp.where(grid > 0.0, within + offset - 1.0, -1.0)


def pick_body(first, ids_hbm, tokens_hbm, *refs):
    picked_ref, peak_ref, ids_ref, tokens_ref, loaded = refs[-5:]
    rows = picked_ref.shape[0]
    count = tokens_ref.shape[0]
    pieces = loaded.shape[0] - 1
    step = count // pieces
    ids_copy = pltpu.make_async_copy(ids_hbm, ids_ref, loaded.at[pieces])
    ids_copy.start()
    copies = [
        pltpu.make_async_copy(
            tokens_hbm.at[pl.ds(i * step, step), :],
            tokens_ref.at[pl.ds(i * step, step), :],
            loaded.at[i],
        )
        for i in range(pieces)
    ]
    for copy in copies:
        copy.start()
    ids_copy.wait()
    slots = slots_of(ids_ref).astype(jnp.int32)
    wanted = iota((rows, LANES), 0) + first
    picked = jnp.zeros(picked_ref.shape, F32)
    for i, copy in enumerate(copies):
        hot = jnp.concatenate(
            [
                jnp.where(wanted == slots[k : k + 1, :], 1.0, 0.0).astype(BF16)
                for k in range(i * step // LANES, (i + 1) * step // LANES)
            ],
            axis=1,
        )
        copy.wait()
        picked += jnp.dot(
            hot, tokens_ref[i * step : (i + 1) * step, :], preferred_element_type=F32
        )
    picked_ref[...] = picked.astype(BF16)
    peak_ref[...] = jnp.broadcast_to(jnp.max(jnp.abs(picked)), peak_ref.shape)


def pick_rows(ids, tokens, first, rows, follow=()):
    count, width = tokens.shape
    blocks = count // LANES
    pieces = math.gcd(blocks, 4)
    in_hbm = [pltpu.with_memory_space_constraint(x, pltpu.HBM) for x in (ids, tokens)]
    return pl.pallas_call(
        lambda *refs: pick_body(first, *refs),
        out_shape=(
            jax.ShapeDtypeStruct((rows, width), BF16),
            jax.ShapeDtypeStruct((8, LANES), F32),
        ),
        in_specs=[pl.BlockSpec(memory_space=pltpu.HBM)] * 2 + follows(follow),
        out_specs=[pl.BlockSpec(memory_space=pltpu.VMEM)] * 2,
        scratch_shapes=[
            pltpu.VMEM(ids.shape, ids.dtype),
            pltpu.VMEM(tokens.shape, tokens.dtype),
            pltpu.SemaphoreType.DMA((pieces + 1,)),
        ],
        compiler_params=params(16),
        cost_estimate=TINY,
        name="pick_rows",
    )(*in_hbm, *follow)


def signs(size):
    common = iota((size, size), 0) & iota((size, size), 1)
    shift = 1
    while shift < size.bit_length():
        shift *= 2
    while shift > 1:
        shift //= 2
        common = common ^ (common >> shift)
    return (1 - 2 * (common & 1)).astype(F32).astype(BF16)


def whole(pieces):
    if len(pieces) == 1:
        return pieces[0][...]
    return jnp.concatenate([piece[...] for piece in pieces], axis=0)


def expand_body(first, cuts, last, me_ref, *refs):
    count = len(cuts)
    parts = []
    for pieces in cuts:
        parts.append(refs[:pieces])
        refs = refs[pieces:]
    before_ref = None
    if last:
        before_ref, refs = refs[0], refs[1:]
    gate_hbm, up_hbm, *outs, total, held, loaded = refs
    width = parts[0][0].shape[1]
    columns = total.shape[2]
    tile = min(256, columns)

    def load(mask):
        rows = pl.ds(pl.multiple_of((me_ref[0] ^ mask) * width, LANES), width)
        return [
            pltpu.make_async_copy(
                weight.at[rows, pl.ds(first, columns)], held.at[mask, at], loaded.at[mask, at]
            )
            for at, weight in enumerate((gate_hbm, up_hbm))
        ]

    loads = [load(mask) for mask in range(count)]
    for copies in loads[:AHEAD]:
        for copy in copies:
            copy.start()
    table = signs(tile)
    for mask, pieces in enumerate(parts):
        for copies in loads[mask + AHEAD : mask + AHEAD + 1]:
            for copy in copies:
                copy.start()
        for at in range(2):
            loads[mask][at].wait()
            term = jnp.dot(whole(pieces), held[mask, at], preferred_element_type=F32)
            if mask == 0:
                total[at] = term
            else:
                total[at] += term
    values = []
    for i in range(columns // tile):
        gate = total[0, :, i * tile : (i + 1) * tile]
        up = total[1, :, i * tile : (i + 1) * tile]
        hidden = (gate * (1.0 / (1.0 + jnp.exp(-gate))) * up).astype(BF16)
        values.append(jnp.dot(hidden, table, preferred_element_type=F32))
        if not last:
            outs[0][i] = values[i]
    if not last:
        return
    values = [before_ref[i] for i in range(before_ref.shape[0])] + values
    steps = len(values)
    gap = 1
    while gap < steps:
        values = [
            values[i] + values[i ^ gap] if not i & gap else values[i ^ gap] - values[i]
            for i in range(steps)
        ]
        gap *= 2
    for i in range(steps):
        low = 0
        for out in outs:
            rows = out.shape[0]
            out[:, i * tile : (i + 1) * tile] = values[i][low : low + rows].astype(BF16)
            low += rows


def expand(parts, rows, me, gate_weight, up_weight, before=None, follow=()):
    depth, width = gate_weight.shape
    last = before is not None
    columns = width // 2
    first = columns if last else 0
    tile = min(256, columns)
    parts = [x if isinstance(x, (list, tuple)) else [x] for x in parts]
    cuts = [len(x) for x in parts]
    parts = [x for pieces in parts for x in pieces]
    count = len(cuts)
    vmem = pl.BlockSpec(memory_space=pltpu.VMEM)
    in_hbm = [pltpu.with_memory_space_constraint(x, pltpu.HBM) for x in (gate_weight, up_weight)]
    args = [me, *parts] + ([before] if last else [])
    used = len(args) + 2
    if last:
        out_shape = [jax.ShapeDtypeStruct((rows // 2, width), BF16)] * 2
    else:
        out_shape = [jax.ShapeDtypeStruct((columns // tile, rows, tile), F32)]
    return pl.pallas_call(
        lambda *refs: expand_body(first, cuts, last, *refs[:used], *refs[used + len(follow) :]),
        in_specs=[pl.BlockSpec(memory_space=pltpu.SMEM)]
        + [vmem] * (used - 3)
        + [pl.BlockSpec(memory_space=pltpu.HBM)] * 2
        + follows(follow),
        out_specs=[vmem] * len(out_shape),
        out_shape=out_shape,
        scratch_shapes=[
            pltpu.VMEM((2, rows, columns), F32),
            pltpu.VMEM((count, 2, depth // count, columns), BF16),
            pltpu.SemaphoreType.DMA((count, 2)),
        ],
        compiler_params=params(EXPAND_MIB),
        cost_estimate=TINY,
        name="expand_last" if last else "expand_first",
    )(*args, *in_hbm, *follow)


def multiply_body(masks, cuts, resumed, last, me_ref, *refs):
    count = len(masks)
    parts = []
    for pieces in cuts:
        parts.append(refs[:pieces])
        refs = refs[pieces:]
    before_ref = None
    if resumed:
        before_ref, refs = refs[0], refs[1:]
    gate_hbm, up_hbm, *outs, held, loaded = refs
    if last:
        *outs, total = outs
    else:
        total = outs[0]
    features = parts[0][0].shape[1]
    width = total.shape[2]

    def load(i):
        rows = pl.ds(pl.multiple_of((me_ref[0] ^ masks[i]) * features, LANES), features)
        return [
            pltpu.make_async_copy(weight.at[rows, :], held.at[i, at], loaded.at[i, at])
            for at, weight in enumerate((gate_hbm, up_hbm))
        ]

    loads = [load(i) for i in range(count)]
    for copies in loads[:AHEAD]:
        for copy in copies:
            copy.start()
    columns = min(512, width)
    for i, pieces in enumerate(parts):
        for copies in loads[i + AHEAD : i + AHEAD + 1]:
            for copy in copies:
                copy.start()
        for at in range(2):
            loads[i][at].wait()
            for low in range(0, width, columns):
                span = slice(low, low + columns)
                term = jnp.dot(whole(pieces), held[i, at, :, span], preferred_element_type=F32)
                if i > 0:
                    term += total[at, :, span]
                elif resumed:
                    term += before_ref[at, :, span]
                total[at, :, span] = term
    if not last:
        return
    tile = min(256, width)
    steps = width // tile
    table = signs(tile)
    values = []
    for i in range(steps):
        gate = total[0, :, i * tile : (i + 1) * tile]
        up = total[1, :, i * tile : (i + 1) * tile]
        hidden = (gate * (1.0 / (1.0 + jnp.exp(-gate))) * up).astype(BF16)
        values.append(jnp.dot(hidden, table, preferred_element_type=F32))
    gap = 1
    while gap < steps:
        values = [
            values[i] + values[i ^ gap] if not i & gap else values[i ^ gap] - values[i]
            for i in range(steps)
        ]
        gap *= 2
    for i in range(steps):
        low = 0
        for out in outs:
            rows = out.shape[0]
            out[:, i * tile : (i + 1) * tile] = values[i][low : low + rows].astype(BF16)
            low += rows


def multiply(parts, me, gate_weight, up_weight, before=None, last=False, follow=()):
    masks = sorted(parts)
    depth, width = gate_weight.shape
    count = len(masks)
    pieces = [x if isinstance(x, (list, tuple)) else [x] for x in (parts[m] for m in masks)]
    cuts = [len(x) for x in pieces]
    rows, features = sum(x.shape[0] for x in pieces[0]), pieces[0][0].shape[1]
    vmem = pl.BlockSpec(memory_space=pltpu.VMEM)
    resumed = before is not None
    in_hbm = [pltpu.with_memory_space_constraint(x, pltpu.HBM) for x in (gate_weight, up_weight)]
    args = [me, *[x for group in pieces for x in group]] + ([before] if resumed else [])
    used = len(args) + 2
    scratch = [
        pltpu.VMEM((count, 2, features, width), BF16),
        pltpu.SemaphoreType.DMA((count, 2)),
    ]
    if last:
        out_shape = [jax.ShapeDtypeStruct((rows // 2, width), BF16)] * 2
        scratch.insert(0, pltpu.VMEM((2, rows, width), F32))
    else:
        out_shape = [jax.ShapeDtypeStruct((2, rows, width), F32)]
    made = pl.pallas_call(
        lambda *refs: multiply_body(
            masks, cuts, resumed, last, *refs[:used], *refs[used + len(follow) :]
        ),
        in_specs=[pl.BlockSpec(memory_space=pltpu.SMEM)]
        + [vmem] * (used - 3)
        + [pl.BlockSpec(memory_space=pltpu.HBM)] * 2
        + follows(follow),
        out_specs=[vmem] * len(out_shape),
        out_shape=out_shape,
        scratch_shapes=scratch,
        compiler_params=params(EXPAND_MIB + 8),
        cost_estimate=TINY,
        name="multiply_last" if last else "multiply",
    )(*args, *in_hbm, *follow)
    return made if last else made[0]


def clip_body(ins, outs):
    level = CLIP_SHARE * jnp.max(ins[0][8:, :])
    low = 0
    for part in ins[1:]:
        rows = part.shape[0]
        outs[0][low : low + rows, :] = jnp.clip(part[...].astype(F32), -level, level).astype(BF16)
        low += rows


def down_body(first, me_ref, clipped_ref, weight_hbm, *refs):
    owners = lax.axis_size("tensor")
    half = owners // 2
    other_ref, same_ref, held, loaded = refs[-4:]
    fc = same_ref.shape[2]
    stride = weight_hbm.shape[1] // owners
    masks = [2 * i + 1 for i in range(half)] + [2 * i for i in range(half)]

    def load(i):
        column = pl.multiple_of((me_ref[0] ^ masks[i]) * stride + first, LANES)
        return pltpu.make_async_copy(
            weight_hbm.at[:, pl.ds(column, fc)],
            held.at[i // 2, :, pl.ds(i % 2 * fc, fc)],
            loaded.at[i],
        )

    loads = [load(i) for i in range(owners)]
    for copy in loads[: 2 * AHEAD]:
        copy.start()
    for pair in range(half):
        for copy in loads[2 * (pair + AHEAD) : 2 * (pair + AHEAD + 1)]:
            copy.start()
        for copy in loads[2 * pair : 2 * pair + 2]:
            copy.wait()
        terms = jnp.dot(clipped_ref[...], held[pair], preferred_element_type=F32).astype(BF16)
        for side in range(2):
            i = 2 * pair + side
            term = terms[:, side * fc : (side + 1) * fc]
            if i < half:
                other_ref[i] = term
            else:
                same_ref[i - half] = term


def down(clipped, weight, me, units, first, follow=()):
    depth = weight.shape[0]
    owners = lax.axis_size("tensor")
    half = owners // 2
    rows = clipped.shape[0]
    fc = units * LANES
    vmem = pl.BlockSpec(memory_space=pltpu.VMEM)
    shape = jax.ShapeDtypeStruct((half, rows, fc), BF16)
    return pl.pallas_call(
        lambda *refs: down_body(first * LANES, *refs),
        in_specs=[
            pl.BlockSpec(memory_space=pltpu.SMEM),
            vmem,
            pl.BlockSpec(memory_space=pltpu.HBM),
        ]
        + follows(follow),
        out_specs=[vmem] * 2,
        out_shape=[shape] * 2,
        scratch_shapes=[
            pltpu.VMEM((half, depth, 2 * fc), BF16),
            pltpu.SemaphoreType.DMA((owners,)),
        ],
        compiler_params=params(16),
        cost_estimate=TINY,
        name="down",
    )(me, clipped, pltpu.with_memory_space_constraint(weight, pltpu.HBM), *follow)


def spread_body(counts, slots_at, ids_ref, probs_ref, *refs):
    out_ref = refs[-1]
    tokens = ids_ref.shape[1]
    summed = []
    for count, slot in zip(counts, slots_at):
        mine, theirs = refs[:count], refs[count : 2 * count]
        refs = refs[2 * count :]
        rows = [(a[0].astype(F32) + b[slot].astype(F32)).astype(BF16) for a, b in zip(mine, theirs)]
        summed.append(jnp.concatenate(rows, axis=0))
    summed = jnp.concatenate(summed, axis=1)
    slots = slots_of(ids_ref)
    share = jnp.where(ids_ref[0:1, :] == 0, probs_ref[0:1, :], 0.0) + jnp.where(
        ids_ref[1:2, :] == 0, probs_ref[1:2, :], 0.0
    )
    blocks = tokens // LANES
    share = jnp.concatenate(
        [share[:, LANES * k : LANES * (k + 1)] for k in range(blocks)]
        + [jnp.zeros((LANES - blocks, LANES), F32)],
        axis=0,
    ).T
    slots = jnp.concatenate(
        [slots, jnp.zeros((LANES - slots.shape[0], LANES), F32)], axis=0
    ).T.astype(jnp.int32)
    at = iota((LANES, summed.shape[0]), 1)
    for k in range(blocks):
        hot = jnp.where(at == slots[:, k : k + 1], 1.0, 0.0).astype(BF16)
        rows = jnp.dot(hot, summed, preferred_element_type=F32)
        out_ref[LANES * k : LANES * (k + 1), :] = (rows * share[:, k : k + 1]).astype(BF16)


def spread(ids, probs, states, slots_at, first, features, out):
    tokens = ids.shape[1]
    fc = sum(state[0][0].shape[2] for state in states)
    args = [ids, probs]
    for state in states:
        args += [x[0] for x in state] + [x[1] for x in state]
    counts = [len(state) for state in states]
    used = len(args)
    in_specs = [pl.BlockSpec(x.shape, lambda i, d=x.ndim: (0,) * d) for x in args]
    earlier = [] if out is None else [out]
    return pl.pallas_call(
        lambda *refs: spread_body(counts, slots_at, *refs[:used], refs[-1]),
        grid=(1,),
        in_specs=in_specs + follows(earlier),
        out_specs=pl.BlockSpec((pl.Element(tokens), pl.Element(fc)), lambda i: (0, first * LANES)),
        out_shape=jax.ShapeDtypeStruct((tokens, features), BF16),
        input_output_aliases={used: 0} if earlier else {},
        compiler_params=params(24),
        cost_estimate=TINY,
        name="spread",
    )(*args, *earlier)


def follows(arrays):
    return [pl.BlockSpec(memory_space=pl.ANY)] * len(arrays)


def small(body, args, shapes, name, follow=()):
    vmem = pl.BlockSpec(memory_space=pltpu.VMEM)
    count = len(args)
    specs = [pl.BlockSpec(memory_space=pltpu.SMEM) if x.ndim == 1 else vmem for x in args]
    return pl.pallas_call(
        lambda *refs: body(refs[:count], refs[count + len(follow) :]),
        in_specs=specs + follows(follow),
        out_specs=[vmem] * len(shapes),
        out_shape=[jax.ShapeDtypeStruct(*x) for x in shapes],
        compiler_params=params(16),
        cost_estimate=TINY,
        name=name,
    )(*args, *follow)


def gather_near(own, orders):
    return {0: own} | {1 << bit: across(own, bit) for bit in orders[0]}


def cut_body(firsts, ins, outs):
    for h, at in enumerate(firsts):
        rows = outs[h].shape[0]
        outs[h][...] = ins[at][h * rows : (h + 1) * rows, :]
    for block, out in zip(ins, outs[2:]):
        out[...] = block[...]


def join_body(ins, outs):
    pieces = 2 * len(outs) // len(ins)
    for i in range(len(ins) // 2):
        whole = jnp.concatenate([ins[2 * i][...], ins[2 * i + 1][...]], axis=0)
        for k in range(pieces):
            out = outs[pieces * i + k]
            rows = out.shape[0]
            out[...] = whole[k * rows : (k + 1) * rows, :]


def cut(full, orders, follow, passed=False):
    rows, width = full[0].shape
    masks = [mask for mask in full if mask]
    firsts = [masks.index(1 << order[0]) for order in orders]
    shapes = [((rows // 2, width), BF16)] * 2 + [((rows, width), BF16)] * len(masks) * passed
    outs = small(
        lambda ins, outs: cut_body(firsts, ins, outs),
        [full[mask] for mask in masks],
        shapes,
        "cut",
        follow,
    )
    return outs[:2], full | dict(zip(masks, outs[2:]))


def gather_far(full, cuts, orders):
    half = full[0].shape[0] // len(orders)
    firsts = [1 << order[0] for order in orders]
    part = {}

    def get(mask, h):
        if (mask, h) in part:
            return part[mask, h]
        return cuts[h] if mask == firsts[h] else full[mask][h * half : (h + 1) * half]

    have = [[0, first] for first in firsts]
    for at in range(1, len(orders[0])):
        for h, order in enumerate(orders):
            bit = order[at]
            for mask in list(have[h]):
                there = mask | 1 << bit
                if there not in full:
                    part[there, h] = across(get(mask, h), bit)
                have[h].append(there)
    return part


def join(part, follow, pieces):
    masks = sorted({mask for mask, _ in part})
    halves = [part[mask, h] for mask in masks for h in range(2)]
    half, width = halves[0].shape
    shapes = [((2 * half // pieces, width), BF16)] * (pieces * len(masks))
    joined = small(join_body, halves, shapes, "join", follow)
    return {mask: joined[pieces * i : pieces * (i + 1)] for i, mask in enumerate(masks)}


def paired(pieces):
    return pieces | {
        mask | 1: [across(x, 0) for x in block] if isinstance(block, list) else across(block, 0)
        for mask, block in pieces.items()
    }


def turn_body(bits, scale, ins, outs):
    me_ref, ins = ins[0], ins[1:]
    count = len(bits)
    for h, bit in enumerate(bits):
        flip = (1 - 2 * ((me_ref[0] >> bit) & 1)).astype(F32)
        own = ins[2 * h][...].astype(F32)
        came = ins[2 * h + 1][...].astype(F32)
        value = came + own * flip
        if scale is not None:
            value = value * scale
            top = jnp.max(jnp.abs(own) + jnp.abs(came), axis=0, keepdims=True) * scale
            wide = top[:, :LANES]
            for k in range(1, top.shape[1] // LANES):
                wide = jnp.maximum(wide, top[:, k * LANES : (k + 1) * LANES])
            outs[count + h][...] = jnp.broadcast_to(wide, outs[count + h].shape)
        outs[h][...] = value.astype(BF16)


def turn(me, blocks, came, bits, follow=(), scale=None):
    args = [me] + [x for pair in zip(blocks, came) for x in pair]
    shapes = [(x.shape, BF16) for x in blocks]
    if scale is not None:
        shapes += [((8, LANES), F32)] * len(blocks)
    return small(
        lambda ins, outs: turn_body(bits, scale, ins, outs), args, shapes, "turn", follow
    )


def largest(top_in, tops, lasts):
    bits = range(lax.axis_size("tensor").bit_length() - 1)
    values = jnp.concatenate([top_in, *tops], axis=0)
    for bit in bits:
        if bit not in lasts:
            values = jnp.maximum(values, across(values, bit))
    n = top_in.shape[0]
    top_in, first, second = values[:n], values[n : 2 * n], values[2 * n :]
    if lasts[0] != lasts[1]:
        pair = jnp.concatenate([top_in, second], axis=0)
        came_first, came_pair = across(first, lasts[1]), across(pair, lasts[0])
        first = jnp.maximum(first, came_first)
        pair = jnp.maximum(pair, came_pair)
        top_in, second = pair[:n], pair[n:]
    values = jnp.concatenate([top_in, jnp.maximum(first, second)], axis=0)
    blocks = lax.axis_size("dp")
    far = 1
    while far < blocks:
        pairs = [(r, r ^ far) for r in range(blocks)]
        values = jnp.maximum(values, lax.ppermute(values, "dp", pairs))
        far *= 2
    return values


def on_device(tokens, expert_ids, gate_probs, gate_weight, up_weight, down_weight):
    count = lax.axis_size("tensor")
    bits = count.bit_length() - 1
    outer = list(range(1, bits))
    orders = [outer, outer[::-1]]
    me = lax.axis_index("tensor")
    me_arr = me.astype(jnp.int32).reshape(1)
    ids, probs = expert_ids.T, gate_probs.T
    rows = CAP // ROW_CHUNKS
    half = rows // 2
    scale = 1.0 / math.sqrt(gate_weight.shape[1] * count)
    stages = [[order[at] for order in orders] for at in range(len(outer))]
    early_bit = stages[-1][1]

    def send(blocks, bits):
        return [across(x, bit) for x, bit in zip(blocks, bits)]

    def start_turn(halves, follow=()):
        blocks = turn(me_arr, halves, send(halves, [0, 0]), [0, 0], follow)
        return blocks, send(blocks, stages[0])

    def go_on(blocks, came, at, follow=()):
        blocks = turn(me_arr, blocks, came, stages[at], follow)
        return blocks, send(blocks, stages[at + 1])

    def end_turn(blocks, came, follow=()):
        made = turn(me_arr, blocks, came, stages[-1], follow, scale)
        return made[: len(blocks)], made[len(blocks) :]

    own_a, top_a = pick_rows(ids, tokens, 0, rows, [me_arr])
    near_a = gather_near(own_a, orders)
    weights = (me_arr, gate_weight, up_weight)
    cuts_a, near_a = cut(near_a, orders, [])
    own_b, top_b = pick_rows(ids, tokens, rows, rows, cuts_a)
    top_in = jnp.maximum(top_a, top_b)
    top_in = jnp.maximum(top_in, across(top_in, early_bit))
    far_a = join(gather_far(near_a, cuts_a, orders), [own_b, top_in], 1)
    near_b = gather_near(own_b, orders)
    parts_a = paired(near_a | far_a)
    parts_a = [parts_a[mask] for mask in range(count)]
    first_a = expand(parts_a, rows, *weights)
    local_a = expand(parts_a, rows, *weights, *first_a)
    cuts_b, near_b = cut(near_b, orders, local_a, True)
    parts_b = paired(near_b)
    theirs_b = [block for mask, block in parts_b.items() if mask & 1]
    blocks_a, came_a = start_turn(local_a, theirs_b)
    total_b = multiply(parts_b, *weights, follow=blocks_a)
    far_b = join(gather_far(near_b, cuts_b, orders), [total_b], 3)
    for at in range(len(outer) - 1):
        blocks_a, came_a = go_on(blocks_a, came_a, at, [total_b])
    local_b = multiply(paired(far_b), *weights, total_b, True, blocks_a)
    turned_a, rot_a = end_turn(blocks_a, came_a, local_b)
    blocks_b, came_b = start_turn(local_b, rot_a)
    for at in range(len(outer) - 1):
        blocks_b, came_b = go_on(blocks_b, came_b, at)
    turned_b, rot_b = end_turn(blocks_b, came_b)
    rotated = turned_a + turned_b

    peaks = largest(top_in, [jnp.maximum(x, y) for x, y in zip(rot_a, rot_b)], stages[-1])
    clipped = small(
        clip_body, [peaks, *rotated], [((CAP, gate_weight.shape[1]), BF16)], "clip"
    )[0]

    tops = pl.pallas_call(
        peaks_body,
        out_specs=pl.BlockSpec(memory_space=pltpu.SMEM),
        out_shape=jax.ShapeDtypeStruct((2,), F32),
        name="peaks",
    )(peaks)
    units = tokens.shape[1] // LANES
    sizes = chunks_of(units)
    firsts = [sum(sizes[:i]) for i in range(len(sizes))]
    total = len(sizes)
    products, begun, ended, out, last = {}, {}, {}, None, []
    for step, chunk in sums_order(total):
        if step == "product":
            products[chunk] = down(
                clipped, down_weight, me_arr, sizes[chunk], firsts[chunk], last
            )
            last = [products[chunk][1]]
        elif step == "begin":
            other, same = products[chunk]
            begun[chunk] = fold_cores(same, across(other, 0), stages[0], last)
            last = [keep for keep, _, _ in begun[chunk]]
        elif step == "finish":
            ahead = [c for c in products if c not in begun]
            passed = [products[c][0] for c in ahead]
            held = chunk == 0 and total > 2
            stacked = [x for _, x, _ in ended[0]] if chunk == 1 and total > 2 else []
            ended[chunk], passed = finish(
                begun[chunk], stages, last, passed, stacked, not held
            )
            if stacked:
                ended[0] = [
                    (keep, both, left)
                    for (keep, _, left), (_, both, _) in zip(ended[0], ended[1])
                ]
            for c, other in zip(ahead, passed):
                products[c] = (other, products[c][1])
            last = [keep for keep, _, _ in ended[chunk]]
        else:
            chunks = [0, 1] if chunk == 0 and total > 2 else [chunk]
            slots_at = [0 if c == 0 else ended[c][0][1].shape[0] - 1 for c in chunks]
            out = spread(
                ids,
                probs,
                [ended[c] for c in chunks],
                slots_at,
                firsts[chunk],
                tokens.shape[1],
                out,
            )
    return out, tops


def chunks_of(units):
    return [2] * (units // 2) + [1] * (units % 2)


def sums_order(total):
    order = [("product", 0)]
    for chunk in range(total):
        if chunk + 1 < total:
            order.append(("product", chunk + 1))
        order.append(("begin", chunk))
        if chunk > 0:
            order.append(("finish", chunk - 1))
    order.append(("finish", total - 1))
    return order + [("spread", c) for c in range(total) if c != 1 or total < 3]


def peaks_body(values_ref, out_ref):
    out_ref[0] = jnp.max(values_ref[:8, :])
    out_ref[1] = jnp.max(values_ref[8:, :])


def fold_body(plan, passed, ins, outs):
    for i in range(passed):
        outs[len(plan) + i][...] = ins[len(ins) - passed + i][...]
    for out, (slots, low) in zip(outs, plan):
        rows = out.shape[1]
        for slot, terms in enumerate(slots):
            total = 0.0
            for at, i in terms:
                total = total + ins[at][i, low : low + rows, :].astype(F32)
            out[slot] = total.astype(BF16)


def fold(args, terms, masks, lows, rows, bits, follow, passed=(), stacked=(), sent=True):
    plan, shapes, lefts = [], [], []
    width = args[0].shape[2]
    for h, bit in enumerate(bits):
        for side in (0, 1):
            chosen = [m for m in masks[h] if m >> bit & 1 == side]
            slots = [terms[h][m] for m in chosen]
            if side and stacked:
                slots = [((len(args) + h, i),) for i in range(stacked[h].shape[0])] + slots
            plan.append((slots, lows[h]))
            shapes.append(((len(slots), rows, width), BF16))
        lefts.append([m for m in masks[h] if not m >> bit & 1])
    shapes += [(x.shape, x.dtype) for x in passed]
    made = small(
        lambda ins, outs: fold_body(plan, len(passed), ins, outs),
        [*args, *stacked, *passed],
        shapes,
        "fold",
        follow,
    )
    state = [
        (made[2 * h], across(made[2 * h + 1], bit) if sent else made[2 * h + 1], lefts[h])
        for h, bit in enumerate(bits)
    ]
    return state, made[len(plan) :]


def fold_cores(same, came, bits, follow):
    half = same.shape[1] // 2
    masks = [2 * i for i in range(same.shape[0])]
    terms = {m: ((0, i), (1, i)) for i, m in enumerate(masks)}
    return fold([same, came], [terms] * 2, [masks] * 2, [0, half], half, bits, follow)[0]


def finish(state, stages, follow, passed=(), stacked=(), sent=True):
    for bits in stages[1:]:
        args = [x for keep, recv, _ in state for x in (keep, recv)]
        masks = [left for _, _, left in state]
        terms = [
            {m: ((2 * h, i), (2 * h + 1, i)) for i, m in enumerate(left)}
            for h, left in enumerate(masks)
        ]
        last = bits is stages[-1]
        state, passed = fold(
            args,
            terms,
            masks,
            [0, 0],
            args[0].shape[1],
            bits,
            follow,
            passed,
            stacked if last else (),
            sent or not last,
        )
    return state, passed


def solution(mesh):
    in_specs = (
        P("dp", "tensor"),
        P("dp", None),
        P("dp", None),
        P(None, "tensor"),
        P(None, "tensor"),
        P("tensor", None),
    )
    out_specs = (P("dp", "tensor"), P())
    return jax.shard_map(
        on_device, mesh=mesh, in_specs=in_specs, out_specs=out_specs, check_vma=False
    )
```

profile of v0, /device:TPU:0, one launch (start us, length us, event | category | flops | bytes accessed | tf_op | source)
XLA Modules:
  0.0 176.8 jit_solution(16525731411602062972)
XLA Ops:
  0.6 3.3 %pick_rows.2 = (bf16[384,768]{1,0:T(8,128)(2,1)S(1)}, f32[8,128]{1,0:T(8,128)S(1)}) custom-call(s32[2,1536]{1,0:T(2,128)} %bitcast.3, bf16[1536,768]{1,0:T(8,128)(2,1)} %refs_1_.3, s32[1]{0:T(128)} %bitcast.2.refs_2_.refs_0_), custom_call_target="tpu_custom_call" | custom-call | flops 1 | bytes 1 | tf_op jit(solution)/shard_map/pick_rows/pallas_call | solution.py:98
  3.9 3.0 %collective-permute-start.1 = (bf16[384,768]{1,0:T(8,128)(2,1)S(1)}, bf16[384,768]{1,0:T(8,128)(2,1)S(1)}, u32[]{:S(2)}, u32[]{:S(2)}) collective-permute-start(bf16[384,768]{1,0:T(8,128)(2,1)S(1)} %get-tuple-element.67.refs_1_), channel_id=1, source_target_pairs={{0,16},{4,20},{8,24},{12,28},{16,0},{20,4},{24,8},{28,12},{1,17},{... | collective-permute-start | bytes 1769480 | tf_op jit(solution)/shard_map/ppermute | solution.py:30
  8.5 11.8 %collective-permute-done.1.refs_1_.refs_5_ = bf16[384,768]{1,0:T(8,128)(2,1)S(1)} collective-permute-done((bf16[384,768]{1,0:T(8,128)(2,1)S(1)}, bf16[384,768]{1,0:T(8,128)(2,1)S(1)}, u32[]{:S(2)}, u32[]{:S(2)}) %collective-permute-start.1) | collective-permute-done | bytes 589856 | tf_op jit(solution)/shard_map/ppermute | solution.py:30
  23.9 3.3 %pick_rows.3 = (bf16[384,768]{1,0:T(8,128)(2,1)S(1)}, f32[8,128]{1,0:T(8,128)S(1)}) custom-call(s32[2,1536]{1,0:T(2,128)} %bitcast.4, bf16[1536,768]{1,0:T(8,128)(2,1)} %refs_1_.3, bf16[192,768]{1,0:T(8,128)(2,1)S(1)} %get-tuple-element.68.refs_2_, bf16[192,768]{1,0:T(8,128)(2,1)S(1)} %get-tuple-element.69.refs_3_), custom_call_target="tpu_custom_call" | custom-call | flops 1 | bytes 1 | tf_op jit(solution)/shard_map/pick_rows/pallas_call | solution.py:98
  27.6 3.2 %collective-permute-done.2 = f32[8,128]{1,0:T(8,128)S(1)} collective-permute-done((f32[8,128]{1,0:T(8,128)S(1)}, f32[8,128]{1,0:T(8,128)S(1)}, u32[]{:S(2)}, u32[]{:S(2)}) %collective-permute-start.2) | collective-permute-done | bytes 4128 | tf_op jit(solution)/shard_map/ppermute | solution.py:30
  33.7 7.4 %expand_first.1.refs_9_ = f32[2,384,256]{2,1,0:T(8,128)S(1)} custom-call(s32[1]{0:T(128)} %bitcast.2.refs_2_.refs_0_, bf16[384,768]{1,0:T(8,128)(2,1)S(1)} %get-tuple-element.67.refs_1_, bf16[384,768]{1,0:T(8,128)(2,1)S(1)} %collective-permute-done.3.refs_2_, bf16[384,768]{1,0:T(8,128)(2,1)S(1)} %collective-permute-done.refs_0_.refs_3_, ...), custom_call_target="tpu_custom_call" | custom-call | flops 1 | bytes 1 | tf_op jit(solution)/shard_map/expand_first/pallas_call | solution.py:218
  41.1 7.4 %expand_last.1 = (bf16[192,1024]{1,0:T(8,128)(2,1)S(1)}, bf16[192,1024]{1,0:T(8,128)(2,1)S(1)}) custom-call(s32[1]{0:T(128)} %bitcast.2.refs_2_.refs_0_, bf16[384,768]{1,0:T(8,128)(2,1)S(1)} %get-tuple-element.67.refs_1_, bf16[384,768]{1,0:T(8,128)(2,1)S(1)} %collective-permute-done.3.refs_2_, bf16[384,768]{1,0:T(8,128)(2,1)S(1)} %collective-permute-done.refs_0_.refs_3_, ...), custom_call_target="tpu_custom_call" | custom-call | flops 1 | bytes 1 | tf_op jit(solution)/shard_map/expand_last/pallas_call | solution.py:218
  55.9 10.8 %multiply.1.refs_5_.refs_2_.refs_7_ = f32[2,384,1024]{2,1,0:T(8,128)S(1)} custom-call(s32[1]{0:T(128)} %bitcast.2.refs_2_.refs_0_, bf16[384,768]{1,0:T(8,128)(2,1)S(1)} %get-tuple-element.71.refs_2_.refs_1_, bf16[384,768]{1,0:T(8,128)(2,1)S(1)} %collective-permute-done.11.refs_5_.refs_2_, bf16[384,768]{1,0:T(8,128)(2,1)S(1)} %get-tuple-element.74.refs_3_, ...), custom_call_target="tpu_custom_call" | custom-call | flops 1 | bytes 1 | tf_op jit(solution)/shard_map/multiply/pallas_call | solution.py:327
  67.5 2.3 %collective-permute-done.16.refs_2_ = bf16[192,1024]{1,0:T(8,128)(2,1)S(1)} collective-permute-done((bf16[192,1024]{1,0:T(8,128)(2,1)S(1)}, bf16[192,1024]{1,0:T(8,128)(2,1)S(1)}, u32[]{:S(2)}, u32[]{:S(2)}) %collective-permute-start.16) | collective-permute-done | bytes 393248 | tf_op jit(solution)/shard_map/ppermute | solution.py:30
  72.1 5.1 %multiply_last.1 = (bf16[192,1024]{1,0:T(8,128)(2,1)S(1)}, bf16[192,1024]{1,0:T(8,128)(2,1)S(1)}) custom-call(s32[1]{0:T(128)} %bitcast.2.refs_2_.refs_0_, bf16[128,768]{1,0:T(8,128)(2,1)S(1)} %get-tuple-element.82.refs_1_, bf16[128,768]{1,0:T(8,128)(2,1)S(1)} %get-tuple-element.83.refs_2_, bf16[128,768]{1,0:T(8,128)(2,1)S(1)} %get-tuple-element.84.refs_3_, ...), custom_call_target="tpu_custom_call" | custom-call | flops 1 | bytes 1 | tf_op jit(solution)/shard_map/multiply_last/pallas_call | solution.py:327
  77.8 2.9 %collective-permute-done.18.refs_2_ = bf16[192,1024]{1,0:T(8,128)(2,1)S(1)} collective-permute-done((bf16[192,1024]{1,0:T(8,128)(2,1)S(1)}, bf16[192,1024]{1,0:T(8,128)(2,1)S(1)}, u32[]{:S(2)}, u32[]{:S(2)}) %collective-permute-start.18) | collective-permute-done | bytes 393248 | tf_op jit(solution)/shard_map/ppermute | solution.py:30
  85.0 6.6 %collective-permute-done.27.refs_2_ = bf16[192,1024]{1,0:T(8,128)(2,1)S(1)} collective-permute-done((bf16[192,1024]{1,0:T(8,128)(2,1)S(1)}, bf16[192,1024]{1,0:T(8,128)(2,1)S(1)}, u32[]{:S(2)}, u32[]{:S(2)}) %collective-permute-start.27) | collective-permute-done | bytes 393248 | tf_op jit(solution)/shard_map/ppermute | solution.py:30
  94.9 6.3 %collective-permute-done.29.refs_2_ = bf16[192,1024]{1,0:T(8,128)(2,1)S(1)} collective-permute-done((bf16[192,1024]{1,0:T(8,128)(2,1)S(1)}, bf16[192,1024]{1,0:T(8,128)(2,1)S(1)}, u32[]{:S(2)}, u32[]{:S(2)}) %collective-permute-start.29) | collective-permute-done | bytes 393248 | tf_op jit(solution)/shard_map/ppermute | solution.py:30
  105.7 2.4 %collective-permute-done.32 = f32[16,128]{1,0:T(8,128)S(1)} collective-permute-done((f32[16,128]{1,0:T(8,128)S(1)}, f32[16,128]{1,0:T(8,128)S(1)}, u32[]{:S(2)}, u32[]{:S(2)}) %collective-permute-start.32) | collective-permute-done | bytes 8224 | tf_op jit(solution)/shard_map/ppermute | solution.py:30
  110.3 2.1 %collective-permute-done.34 = f32[16,128]{1,0:T(8,128)S(1)} collective-permute-done((f32[16,128]{1,0:T(8,128)S(1)}, f32[16,128]{1,0:T(8,128)S(1)}, u32[]{:S(2)}, u32[]{:S(2)}) %collective-permute-start.34) | collective-permute-done | bytes 8224 | tf_op jit(solution)/shard_map/ppermute | solution.py:610
  112.4 2.6 %collective-permute-start.35 = (f32[16,128]{1,0:T(8,128)S(1)}, f32[16,128]{1,0:T(8,128)S(1)}, u32[]{:S(2)}, u32[]{:S(2)}) collective-permute-start(f32[16,128]{1,0:T(8,128)S(1)} %fusion), channel_id=1, source_target_pairs={{0,2},{1,3},{2,0},{3,1},{4,6},{5,7},{6,4},{7,5},{8,10},{9,11},{10,... | collective-permute-start | bytes 24584 | tf_op jit(solution)/shard_map/ppermute | solution.py:610
  117.5 5.5 %down.3 = (bf16[4,768,256]{2,1,0:T(8,128)(2,1)S(1)}, bf16[4,768,256]{2,1,0:T(8,128)(2,1)S(1)}) custom-call(s32[1]{0:T(128)} %bitcast.2.refs_2_.refs_0_, bf16[768,1024]{1,0:T(8,128)(2,1)S(1)} %clip.1.refs_1_, bf16[1024,6144]{1,0:T(8,128)(2,1)} %refs_2_.5), custom_call_target="tpu_custom_call" | custom-call | flops 1 | bytes 1 | tf_op jit(solution)/shard_map/down/pallas_call | solution.py:396
  123.1 5.2 %down.4 = (bf16[4,768,256]{2,1,0:T(8,128)(2,1)S(1)}, bf16[4,768,256]{2,1,0:T(8,128)(2,1)S(1)}) custom-call(s32[1]{0:T(128)} %bitcast.2.refs_2_.refs_0_, bf16[768,1024]{1,0:T(8,128)(2,1)S(1)} %clip.1.refs_1_, bf16[1024,6144]{1,0:T(8,128)(2,1)} %refs_2_.5, bf16[4,768,256]{2,1,0:T(8,128)(2,1)S(1)} %get-tuple-element.99.refs_3_.refs_0_), custom_call_target="tpu_custom_call" | custom-call | flops 1 | bytes 1 | tf_op jit(solution)/shard_map/down/pallas_call | solution.py:396
  131.2 5.2 %down.5 = (bf16[4,768,256]{2,1,0:T(8,128)(2,1)S(1)}, bf16[4,768,256]{2,1,0:T(8,128)(2,1)S(1)}) custom-call(s32[1]{0:T(128)} %bitcast.2.refs_2_.refs_0_, bf16[768,1024]{1,0:T(8,128)(2,1)S(1)} %clip.1.refs_1_, bf16[1024,6144]{1,0:T(8,128)(2,1)} %refs_2_.5, bf16[2,384,256]{2,1,0:T(8,128)(2,1)S(1)} %get-tuple-element.102.refs_3_.refs_0_, ...), custom_call_target="tpu_custom_call" | custom-call | flops 1 | bytes 1 | tf_op jit(solution)/shard_map/down/pallas_call | solution.py:396
  136.8 3.5 %collective-permute-done.37.refs_1_ = bf16[2,384,256]{2,1,0:T(8,128)(2,1)S(1)} collective-permute-done((bf16[2,384,256]{2,1,0:T(8,128)(2,1)S(1)}, bf16[2,384,256]{2,1,0:T(8,128)(2,1)S(1)}, u32[]{:S(2)}, u32[]{:S(2)}) %collective-permute-start.37) | collective-permute-done | bytes 393248 | tf_op jit(solution)/shard_map/ppermute | solution.py:30
  147.6 5.4 %collective-permute-done.43.refs_1_ = bf16[2,384,256]{2,1,0:T(8,128)(2,1)S(1)} collective-permute-done((bf16[2,384,256]{2,1,0:T(8,128)(2,1)S(1)}, bf16[2,384,256]{2,1,0:T(8,128)(2,1)S(1)}, u32[]{:S(2)}, u32[]{:S(2)}) %collective-permute-start.43) | collective-permute-done | bytes 393248 | tf_op jit(solution)/shard_map/ppermute | solution.py:30
  156.7 4.7 %collective-permute-done.41.refs_1_ = bf16[2,384,256]{2,1,0:T(8,128)(2,1)S(1)} collective-permute-done((bf16[2,384,256]{2,1,0:T(8,128)(2,1)S(1)}, bf16[2,384,256]{2,1,0:T(8,128)(2,1)S(1)}, u32[]{:S(2)}, u32[]{:S(2)}) %collective-permute-start.41) | collective-permute-done | bytes 393248 | tf_op jit(solution)/shard_map/ppermute | solution.py:30
  167.0 4.4 %collective-permute-done.47.refs_4_.refs_8_ = bf16[2,384,256]{2,1,0:T(8,128)(2,1)S(1)} collective-permute-done((bf16[2,384,256]{2,1,0:T(8,128)(2,1)S(1)}, bf16[2,384,256]{2,1,0:T(8,128)(2,1)S(1)}, u32[]{:S(2)}, u32[]{:S(2)}) %collective-permute-start.47) | collective-permute-done | bytes 393248 | tf_op jit(solution)/shard_map/ppermute | solution.py:30
  171.4 2.9 %spread.2.refs_6_ = bf16[1536,768]{1,0:T(8,128)(2,1)} custom-call(s32[2,1536]{1,0:T(2,128)S(1)} %bitcast.5, f32[2,1536]{1,0:T(2,128)S(1)} %bitcast.7, bf16[1,384,256]{2,1,0:T(8,128)(2,1)S(1)} %get-tuple-element.112.refs_2_, bf16[1,384,256]{2,1,0:T(8,128)(2,1)S(1)} %get-tuple-element.113.refs_3_, ...), custom_call_target="tpu_custom_call" | custom-call | flops 1 | bytes 1 | tf_op jit(solution)/shard_map/spread/pallas_call | solution.py:456
  (122 shorter events, 58.4 us)
Async XLA Ops:
  3.9 16.4 %collective-permute-start.1 = (bf16[384,768]{1,0:T(8,128)(2,1)S(1)}, bf16[384,768]{1,0:T(8,128)(2,1)S(1)}, u32[]{:S(2)}, u32[]{:S(2)}) collective-permute-start(bf16[384,768]{1,0:T(8,128)(2,1)S(1)} %get-tuple-element.67.refs_1_), channel_id=1, source_target_pairs={{0,16},{4,20},{8,24},{12,28},{16,0},{20,4},{24,8},{28,12},{1,17},{... | collective-permute-start | bytes 1769480 | tf_op jit(solution)/shard_map/ppermute | solution.py:30
  7.0 14.8 %collective-permute-start = (bf16[384,768]{1,0:T(8,128)(2,1)S(1)}, bf16[384,768]{1,0:T(8,128)(2,1)S(1)}, u32[]{:S(2)}, u32[]{:S(2)}) collective-permute-start(bf16[384,768]{1,0:T(8,128)(2,1)S(1)} %get-tuple-element.67.refs_1_), channel_id=1, source_target_pairs={{0,8},{4,12},{8,0},{12,4},{16,24},{20,28},{24,16},{28,20},{1,9},{5... | collective-permute-start | bytes 1769480 | tf_op jit(solution)/shard_map/ppermute | solution.py:30
  8.5 24.5 %collective-permute-start.3 = (bf16[384,768]{1,0:T(8,128)(2,1)S(1)}, bf16[384,768]{1,0:T(8,128)(2,1)S(1)}, u32[]{:S(2)}, u32[]{:S(2)}) collective-permute-start(bf16[384,768]{1,0:T(8,128)(2,1)S(1)} %get-tuple-element.67.refs_1_), channel_id=1, source_target_pairs={{0,4},{4,0},{8,12},{12,8},{16,20},{20,16},{24,28},{28,24},{1,5},{5... | collective-permute-start | bytes 1769480 | tf_op jit(solution)/shard_map/ppermute | solution.py:30
  23.9 9.7 %collective-permute-start.5 = (bf16[384,768]{1,0:T(8,128)(2,1)S(1)}, bf16[384,768]{1,0:T(8,128)(2,1)S(1)}, u32[]{:S(2)}, u32[]{:S(2)}) collective-permute-start(bf16[384,768]{1,0:T(8,128)(2,1)S(1)} %collective-permute-done.1.refs_1_.refs_5_), channel_id=1, source_target_pairs={{0,4},{4,0},{8,12},{12,8},{16,20},{20,16},{24,28},{28,24},{1,5},{5... | collective-permute-start | bytes 1769480 | tf_op jit(solution)/shard_map/ppermute | solution.py:30
  31.5 17.0 %collective-permute-start.13 = (bf16[384,768]{1,0:T(8,128)(2,1)S(1)}, bf16[384,768]{1,0:T(8,128)(2,1)S(1)}, u32[]{:S(2)}, u32[]{:S(2)}) collective-permute-start(bf16[384,768]{1,0:T(8,128)(2,1)S(1)} %get-tuple-element.71.refs_2_.refs_1_), channel_id=1, source_target_pairs={{0,16},{4,20},{8,24},{12,28},{16,0},{20,4},{24,8},{28,12},{1,17},{... | collective-permute-start | bytes 1769480 | tf_op jit(solution)/shard_map/ppermute | solution.py:30
  33.0 15.5 %collective-permute-start.12 = (bf16[384,768]{1,0:T(8,128)(2,1)S(1)}, bf16[384,768]{1,0:T(8,128)(2,1)S(1)}, u32[]{:S(2)}, u32[]{:S(2)}) collective-permute-start(bf16[384,768]{1,0:T(8,128)(2,1)S(1)} %get-tuple-element.71.refs_2_.refs_1_), channel_id=1, source_target_pairs={{0,8},{4,12},{8,0},{12,4},{16,24},{20,28},{24,16},{28,20},{1,9},{5... | collective-permute-start | bytes 1769480 | tf_op jit(solution)/shard_map/ppermute | solution.py:30
  33.5 16.2 %collective-permute-start.11 = (bf16[384,768]{1,0:T(8,128)(2,1)S(1)}, bf16[384,768]{1,0:T(8,128)(2,1)S(1)}, u32[]{:S(2)}, u32[]{:S(2)}) collective-permute-start(bf16[384,768]{1,0:T(8,128)(2,1)S(1)} %get-tuple-element.71.refs_2_.refs_1_), channel_id=1, source_target_pairs={{0,4},{4,0},{8,12},{12,8},{16,20},{20,16},{24,28},{28,24},{1,5},{5... | collective-permute-start | bytes 1769480 | tf_op jit(solution)/shard_map/ppermute | solution.py:30
  49.7 17.1 %collective-permute-start.20 = (bf16[192,768]{1,0:T(8,128)(2,1)S(1)}, bf16[192,768]{1,0:T(8,128)(2,1)S(1)}, u32[]{:S(2)}, u32[]{:S(2)}) collective-permute-start(bf16[192,768]{1,0:T(8,128)(2,1)S(1)} %get-tuple-element.80), channel_id=1, source_target_pairs={{0,16},{4,20},{8,24},{12,28},{16,0},{20,4},{24,8},{28,12},{1,17},{... | collective-permute-start | bytes 884744 | tf_op jit(solution)/shard_map/ppermute | solution.py:30
  52.1 14.7 %collective-permute-start.21 = (bf16[192,768]{1,0:T(8,128)(2,1)S(1)}, bf16[192,768]{1,0:T(8,128)(2,1)S(1)}, u32[]{:S(2)}, u32[]{:S(2)}) collective-permute-start(bf16[192,768]{1,0:T(8,128)(2,1)S(1)} %get-tuple-element.81), channel_id=1, source_target_pairs={{0,8},{4,12},{8,0},{12,4},{16,24},{20,28},{24,16},{28,20},{1,9},{5... | collective-permute-start | bytes 884744 | tf_op jit(solution)/shard_map/ppermute | solution.py:30
  53.8 16.0 %collective-permute-start.16 = (bf16[192,1024]{1,0:T(8,128)(2,1)S(1)}, bf16[192,1024]{1,0:T(8,128)(2,1)S(1)}, u32[]{:S(2)}, u32[]{:S(2)}) collective-permute-start(bf16[192,1024]{1,0:T(8,128)(2,1)S(1)} %get-tuple-element.76.refs_9_.refs_1_), channel_id=1, source_target_pairs={{0,8},{4,12},{8,0},{12,4},{16,24},{20,28},{24,16},{28,20},{1,9},{5... | collective-permute-start | bytes 1179656 | tf_op jit(solution)/shard_map/ppermute | solution.py:30
  54.5 15.3 %collective-permute-start.17 = (bf16[192,1024]{1,0:T(8,128)(2,1)S(1)}, bf16[192,1024]{1,0:T(8,128)(2,1)S(1)}, u32[]{:S(2)}, u32[]{:S(2)}) collective-permute-start(bf16[192,1024]{1,0:T(8,128)(2,1)S(1)} %get-tuple-element.77.refs_10_.refs_3_), channel_id=1, source_target_pairs={{0,16},{4,20},{8,24},{12,28},{16,0},{20,4},{24,8},{28,12},{1,17},{... | collective-permute-start | bytes 1179656 | tf_op jit(solution)/shard_map/ppermute | solution.py:30
  70.0 10.6 %collective-permute-start.18 = (bf16[192,1024]{1,0:T(8,128)(2,1)S(1)}, bf16[192,1024]{1,0:T(8,128)(2,1)S(1)}, u32[]{:S(2)}, u32[]{:S(2)}) collective-permute-start(bf16[192,1024]{1,0:T(8,128)(2,1)S(1)} %get-tuple-element.78.refs_10_.refs_1_), channel_id=1, source_target_pairs={{0,16},{4,20},{8,24},{12,28},{16,0},{20,4},{24,8},{28,12},{1,17},{... | collective-permute-start | bytes 1179656 | tf_op jit(solution)/shard_map/ppermute | solution.py:30
  71.4 10.0 %collective-permute-start.19 = (bf16[192,1024]{1,0:T(8,128)(2,1)S(1)}, bf16[192,1024]{1,0:T(8,128)(2,1)S(1)}, u32[]{:S(2)}, u32[]{:S(2)}) collective-permute-start(bf16[192,1024]{1,0:T(8,128)(2,1)S(1)} %get-tuple-element.79.refs_11_.refs_3_), channel_id=1, source_target_pairs={{0,8},{4,12},{8,0},{12,4},{16,24},{20,28},{24,16},{28,20},{1,9},{5... | collective-permute-start | bytes 1179656 | tf_op jit(solution)/shard_map/ppermute | solution.py:30
  83.4 9.2 %collective-permute-start.28 = (bf16[192,1024]{1,0:T(8,128)(2,1)S(1)}, bf16[192,1024]{1,0:T(8,128)(2,1)S(1)}, u32[]{:S(2)}, u32[]{:S(2)}) collective-permute-start(bf16[192,1024]{1,0:T(8,128)(2,1)S(1)} %get-tuple-element.90.refs_3_), channel_id=1, source_target_pairs={{0,16},{4,20},{8,24},{12,28},{16,0},{20,4},{24,8},{28,12},{1,17},{... | collective-permute-start | bytes 1179656 | tf_op jit(solution)/shard_map/ppermute | solution.py:30
  129.3 11.1 %collective-permute-start.37 = (bf16[2,384,256]{2,1,0:T(8,128)(2,1)S(1)}, bf16[2,384,256]{2,1,0:T(8,128)(2,1)S(1)}, u32[]{:S(2)}, u32[]{:S(2)}) collective-permute-start(bf16[2,384,256]{2,1,0:T(8,128)(2,1)S(1)} %get-tuple-element.105), channel_id=1, source_target_pairs={{0,8},{4,12},{8,0},{12,4},{16,24},{20,28},{24,16},{28,20},{1,9},{5... | collective-permute-start | bytes 1179656 | tf_op jit(solution)/shard_map/ppermute | solution.py:30
  129.9 10.8 %collective-permute-start.38 = (bf16[2,384,256]{2,1,0:T(8,128)(2,1)S(1)}, bf16[2,384,256]{2,1,0:T(8,128)(2,1)S(1)}, u32[]{:S(2)}, u32[]{:S(2)}) collective-permute-start(bf16[2,384,256]{2,1,0:T(8,128)(2,1)S(1)} %get-tuple-element.106), channel_id=1, source_target_pairs={{0,16},{4,20},{8,24},{12,28},{16,0},{20,4},{24,8},{28,12},{1,17},{... | collective-permute-start | bytes 1179656 | tf_op jit(solution)/shard_map/ppermute | solution.py:30
  141.0 12.0 %collective-permute-start.43 = (bf16[2,384,256]{2,1,0:T(8,128)(2,1)S(1)}, bf16[2,384,256]{2,1,0:T(8,128)(2,1)S(1)}, u32[]{:S(2)}, u32[]{:S(2)}) collective-permute-start(bf16[2,384,256]{2,1,0:T(8,128)(2,1)S(1)} %get-tuple-element.118), channel_id=1, source_target_pairs={{0,8},{4,12},{8,0},{12,4},{16,24},{20,28},{24,16},{28,20},{1,9},{5... | collective-permute-start | bytes 1179656 | tf_op jit(solution)/shard_map/ppermute | solution.py:30
  142.5 12.0 %collective-permute-start.44 = (bf16[2,384,256]{2,1,0:T(8,128)(2,1)S(1)}, bf16[2,384,256]{2,1,0:T(8,128)(2,1)S(1)}, u32[]{:S(2)}, u32[]{:S(2)}) collective-permute-start(bf16[2,384,256]{2,1,0:T(8,128)(2,1)S(1)} %get-tuple-element.119), channel_id=1, source_target_pairs={{0,16},{4,20},{8,24},{12,28},{16,0},{20,4},{24,8},{28,12},{1,17},{... | collective-permute-start | bytes 1179656 | tf_op jit(solution)/shard_map/ppermute | solution.py:30
  144.8 16.6 %collective-permute-start.41 = (bf16[2,384,256]{2,1,0:T(8,128)(2,1)S(1)}, bf16[2,384,256]{2,1,0:T(8,128)(2,1)S(1)}, u32[]{:S(2)}, u32[]{:S(2)}) collective-permute-start(bf16[2,384,256]{2,1,0:T(8,128)(2,1)S(1)} %get-tuple-element.115), channel_id=1, source_target_pairs={{0,8},{4,12},{8,0},{12,4},{16,24},{20,28},{24,16},{28,20},{1,9},{5... | collective-permute-start | bytes 1179656 | tf_op jit(solution)/shard_map/ppermute | solution.py:30
  146.3 16.6 %collective-permute-start.42 = (bf16[2,384,256]{2,1,0:T(8,128)(2,1)S(1)}, bf16[2,384,256]{2,1,0:T(8,128)(2,1)S(1)}, u32[]{:S(2)}, u32[]{:S(2)}) collective-permute-start(bf16[2,384,256]{2,1,0:T(8,128)(2,1)S(1)} %get-tuple-element.117), channel_id=1, source_target_pairs={{0,16},{4,20},{8,24},{12,28},{16,0},{20,4},{24,8},{28,12},{1,17},{... | collective-permute-start | bytes 1179656 | tf_op jit(solution)/shard_map/ppermute | solution.py:30
  154.7 16.6 %collective-permute-start.47 = (bf16[2,384,256]{2,1,0:T(8,128)(2,1)S(1)}, bf16[2,384,256]{2,1,0:T(8,128)(2,1)S(1)}, u32[]{:S(2)}, u32[]{:S(2)}) collective-permute-start(bf16[2,384,256]{2,1,0:T(8,128)(2,1)S(1)} %get-tuple-element.128), channel_id=1, source_target_pairs={{0,16},{4,20},{8,24},{12,28},{16,0},{20,4},{24,8},{28,12},{1,17},{... | collective-permute-start | bytes 1179656 | tf_op jit(solution)/shard_map/ppermute | solution.py:30
  156.1 15.2 %collective-permute-start.48 = (bf16[2,384,256]{2,1,0:T(8,128)(2,1)S(1)}, bf16[2,384,256]{2,1,0:T(8,128)(2,1)S(1)}, u32[]{:S(2)}, u32[]{:S(2)}) collective-permute-start(bf16[2,384,256]{2,1,0:T(8,128)(2,1)S(1)} %get-tuple-element.129), channel_id=1, source_target_pairs={{0,8},{4,12},{8,0},{12,4},{16,24},{20,28},{24,16},{28,20},{1,9},{5... | collective-permute-start | bytes 1179656 | tf_op jit(solution)/shard_map/ppermute | solution.py:30
  163.7 11.1 %collective-permute-start.45 = (bf16[1,384,256]{2,1,0:T(8,128)(2,1)}, bf16[1,384,256]{2,1,0:T(8,128)(2,1)S(1)}, u32[]{:S(2)}, u32[]{:S(2)}) collective-permute-start(bf16[1,384,256]{2,1,0:T(8,128)(2,1)} %get-tuple-element.126), channel_id=1, source_target_pairs={{0,16},{4,20},{8,24},{12,28},{16,0},{20,4},{24,8},{28,12},{1,17},{... | collective-permute-start | bytes 589832 | tf_op jit(solution)/shard_map/ppermute | solution.py:30
  165.0 9.7 %collective-permute-start.46 = (bf16[1,384,256]{2,1,0:T(8,128)(2,1)S(1)}, bf16[1,384,256]{2,1,0:T(8,128)(2,1)S(1)}, u32[]{:S(2)}, u32[]{:S(2)}) collective-permute-start(bf16[1,384,256]{2,1,0:T(8,128)(2,1)S(1)} %get-tuple-element.127), channel_id=1, source_target_pairs={{0,8},{4,12},{8,0},{12,4},{16,24},{20,28},{24,16},{28,20},{1,9},{5... | collective-permute-start | bytes 589832 | tf_op jit(solution)/shard_map/ppermute | solution.py:30
  (28 other events, 161.9 us)
where the time goes:
time: 177 us
  waiting for transfers between devices  69.1 us (39%)
  Pallas kernels  65.1 us (37%)
  starting transfers between devices  41.6 us (24%)
    ppermute x47, waiting for transfers between devices, across(): lax.ppermute(block, 'tensor', [(r, r ^ 1 << bit) for r in range(count)])  65.1 us
    ppermute x47, starting transfers between devices, across(): lax.ppermute(block, 'tensor', [(r, r ^ 1 << bit) for r in range(count)])  37.4 us
    pallas_call x3, Pallas kernels, down(): pl.pallas_call(lambda *refs: down_body(first * LANES, *refs), in_specs=[p...  15.9 us
    pallas_call x2, Pallas kernels, multiply(): pl.pallas_call(lambda *refs: multiply_body(masks, cuts, resumed, last, *r...  15.9 us
    pallas_call x2, Pallas kernels, expand(): pl.pallas_call(lambda *refs: expand_body(first, cuts, last, *refs[:used],...  14.8 us
    pallas_call x2, Pallas kernels, pick_rows(): pl.pallas_call(lambda *refs: pick_body(first, *refs), out_shape=(jax.Shap...  6.56 us
    pallas_call x17, Pallas kernels, small(): pl.pallas_call(lambda *refs: body(refs[:count], refs[count + len(follow):...  5.62 us
    pallas_call x2, Pallas kernels, spread(): pl.pallas_call(lambda *refs: spread_body(counts, slots_at, *refs[:used],...  4.96 us
  transfers between devices with their start and end apart: 49, of which 26 were waited for; matrix products, arithmetic and copies ran while one was open for 0% of the time, Pallas kernels for 30%

commit v1 on v0

--- a/solution.py
+++ b/solution.py
@@ -342,16 +342,23 @@
     return made if last else made[0]
 
 
-def clip_body(ins, outs):
-    level = CLIP_SHARE * jnp.max(ins[0][8:, :])
+def clip_rows(peaks_ref, rotated, clipped_ref):
+    level = CLIP_SHARE * jnp.max(peaks_ref[8:, :])
     low = 0
-    for part in ins[1:]:
+    for part in rotated:
         rows = part.shape[0]
-        outs[0][low : low + rows, :] = jnp.clip(part[...].astype(F32), -level, level).astype(BF16)
+        clipped_ref[low : low + rows, :] = jnp.clip(
+            part[...].astype(F32), -level, level
+        ).astype(BF16)
         low += rows
 
 
-def down_body(first, me_ref, clipped_ref, weight_hbm, *refs):
+def down_body(first, fresh, me_ref, *refs):
+    if fresh:
+        peaks_ref, rotated, weight_hbm = refs[0], refs[1:fresh], refs[fresh]
+        clipped_ref, refs = refs[-5], refs[:-5] + refs[-4:]
+    else:
+        clipped_ref, weight_hbm = refs[:2]
     owners = lax.axis_size("tensor")
     half = owners // 2
     other_ref, same_ref, held, loaded = refs[-4:]
@@ -370,6 +377,8 @@
     loads = [load(i) for i in range(owners)]
     for copy in loads[: 2 * AHEAD]:
         copy.start()
+    if fresh:
+        clip_rows(peaks_ref, rotated, clipped_ref)
     for pair in range(half):
         for copy in loads[2 * (pair + AHEAD) : 2 * (pair + AHEAD + 1)]:
             copy.start()
@@ -385,24 +394,24 @@
                 same_ref[i - half] = term
 
 
-def down(clipped, weight, me, units, first, follow=()):
+def down(clipped, weight, me, units, first, follow=(), fresh=()):
     depth = weight.shape[0]
     owners = lax.axis_size("tensor")
     half = owners // 2
-    rows = clipped.shape[0]
+    args = list(fresh) if fresh else [clipped]
+    rows = sum(x.shape[0] for x in (fresh[1:] if fresh else [clipped]))
     fc = units * LANES
     vmem = pl.BlockSpec(memory_space=pltpu.VMEM)
-    shape = jax.ShapeDtypeStruct((half, rows, fc), BF16)
+    shapes = [jax.ShapeDtypeStruct((rows, depth), BF16)] * bool(fresh)
+    shapes += [jax.ShapeDtypeStruct((half, rows, fc), BF16)] * 2
     return pl.pallas_call(
-        lambda *refs: down_body(first * LANES, *refs),
-        in_specs=[
-            pl.BlockSpec(memory_space=pltpu.SMEM),
-            vmem,
-            pl.BlockSpec(memory_space=pltpu.HBM),
-        ]
+        lambda *refs: down_body(first * LANES, len(fresh), *refs),
+        in_specs=[pl.BlockSpec(memory_space=pltpu.SMEM)]
+        + [vmem] * len(args)
+        + [pl.BlockSpec(memory_space=pltpu.HBM)]
         + follows(follow),
-        out_specs=[vmem] * 2,
-        out_shape=[shape] * 2,
+        out_specs=[vmem] * len(shapes),
+        out_shape=shapes,
         scratch_shapes=[
             pltpu.VMEM((half, depth, 2 * fc), BF16),
             pltpu.SemaphoreType.DMA((owners,)),
@@ -410,7 +419,7 @@
         compiler_params=params(16),
         cost_estimate=TINY,
         name="down",
-    )(me, clipped, pltpu.with_memory_space_constraint(weight, pltpu.HBM), *follow)
+    )(me, *args, pltpu.with_memory_space_constraint(weight, pltpu.HBM), *follow)
 
 
 def spread_body(counts, slots_at, ids_ref, probs_ref, *refs):
@@ -671,10 +680,6 @@
     rotated = turned_a + turned_b
 
     peaks = largest(top_in, [jnp.maximum(x, y) for x, y in zip(rot_a, rot_b)], stages[-1])
-    clipped = small(
-        clip_body, [peaks, *rotated], [((CAP, gate_weight.shape[1]), BF16)], "clip"
-    )[0]
-
     tops = pl.pallas_call(
         peaks_body,
         out_specs=pl.BlockSpec(memory_space=pltpu.SMEM),
@@ -685,12 +690,14 @@
     sizes = chunks_of(units)
     firsts = [sum(sizes[:i]) for i in range(len(sizes))]
     total = len(sizes)
-    products, begun, ended, out, last = {}, {}, {}, None, []
+    products, begun, ended, out, last, clipped = {}, {}, {}, None, [], None
     for step, chunk in sums_order(total):
         if step == "product":
-            products[chunk] = down(
-                clipped, down_weight, me_arr, sizes[chunk], firsts[chunk], last
-            )
+            fresh = [peaks, *rotated] if chunk == 0 else []
+            made = down(clipped, down_weight, me_arr, sizes[chunk], firsts[chunk], last, fresh)
+            if fresh:
+                clipped, made = made[0], made[1:]
+            products[chunk] = made
             last = [products[chunk][1]]
         elif step == "begin":
             other, same = products[chunk]

time: 177 us -> 177 us (level)
    pallas_call x17 -> x16, Pallas kernels: 5.62 us -> 5.06 us  [small(): pl.pallas_call(lambda *refs: body(refs[:count], refs[count + len(follow):...]
where the time goes in v1:
time: 177 us; the launch traced here: 176 us
  waiting for transfers between devices  69 us (39%)
  Pallas kernels  64.5 us (36%)
  starting transfers between devices  41.6 us (24%)
    ppermute x47, waiting for transfers between devices, across(): lax.ppermute(block, 'tensor', [(r, r ^ 1 << bit) for r in range(count)])  65 us
    ppermute x47, starting transfers between devices, across(): lax.ppermute(block, 'tensor', [(r, r ^ 1 << bit) for r in range(count)])  37.4 us
    pallas_call x3, Pallas kernels, down(): pl.pallas_call(lambda *refs: down_body(first * LANES, len(fresh), *refs),...  15.9 us
    pallas_call x2, Pallas kernels, multiply(): pl.pallas_call(lambda *refs: multiply_body(masks, cuts, resumed, last, *r...  15.9 us
    pallas_call x2, Pallas kernels, expand(): pl.pallas_call(lambda *refs: expand_body(first, cuts, last, *refs[:used],...  14.8 us
    pallas_call x2, Pallas kernels, pick_rows(): pl.pallas_call(lambda *refs: pick_body(first, *refs), out_shape=(jax.Shap...  6.56 us
    pallas_call x16, Pallas kernels, small(): pl.pallas_call(lambda *refs: body(refs[:count], refs[count + len(follow):...  5.06 us
    pallas_call x2, Pallas kernels, spread(): pl.pallas_call(lambda *refs: spread_body(counts, slots_at, *refs[:used],...  4.96 us
  transfers between devices with their start and end apart: 49, of which 26 were waited for; matrix products, arithmetic and copies ran while one was open for 0% of the time, Pallas kernels for 30%

profile of v1, /device:TPU:0, one launch (start us, length us, event | category | flops | bytes accessed | tf_op | source)
XLA Modules:
  0.0 176.2 jit_solution(11903899310811139913)
XLA Ops:
  0.6 3.3 %pick_rows.2 = (bf16[384,768]{1,0:T(8,128)(2,1)S(1)}, f32[8,128]{1,0:T(8,128)S(1)}) custom-call(s32[2,1536]{1,0:T(2,128)} %bitcast.3, bf16[1536,768]{1,0:T(8,128)(2,1)} %refs_1_.3, s32[1]{0:T(128)} %bitcast.2.refs_2_.refs_0_), custom_call_target="tpu_custom_call" | custom-call | flops 1 | bytes 1 | tf_op jit(solution)/shard_map/pick_rows/pallas_call | solution.py:98
  3.9 3.0 %collective-permute-start.1 = (bf16[384,768]{1,0:T(8,128)(2,1)S(1)}, bf16[384,768]{1,0:T(8,128)(2,1)S(1)}, u32[]{:S(2)}, u32[]{:S(2)}) collective-permute-start(bf16[384,768]{1,0:T(8,128)(2,1)S(1)} %get-tuple-element.68.refs_1_), channel_id=1, source_target_pairs={{0,16},{4,20},{8,24},{12,28},{16,0},{20,4},{24,8},{28,12},{1,17},{... | collective-permute-start | bytes 1769480 | tf_op jit(solution)/shard_map/ppermute | solution.py:30
  8.5 11.8 %collective-permute-done.1.refs_1_.refs_5_ = bf16[384,768]{1,0:T(8,128)(2,1)S(1)} collective-permute-done((bf16[384,768]{1,0:T(8,128)(2,1)S(1)}, bf16[384,768]{1,0:T(8,128)(2,1)S(1)}, u32[]{:S(2)}, u32[]{:S(2)}) %collective-permute-start.1) | collective-permute-done | bytes 589856 | tf_op jit(solution)/shard_map/ppermute | solution.py:30
  23.9 3.3 %pick_rows.3 = (bf16[384,768]{1,0:T(8,128)(2,1)S(1)}, f32[8,128]{1,0:T(8,128)S(1)}) custom-call(s32[2,1536]{1,0:T(2,128)} %bitcast.4, bf16[1536,768]{1,0:T(8,128)(2,1)} %refs_1_.3, bf16[192,768]{1,0:T(8,128)(2,1)S(1)} %get-tuple-element.69.refs_2_, bf16[192,768]{1,0:T(8,128)(2,1)S(1)} %get-tuple-element.70.refs_3_), custom_call_target="tpu_custom_call" | custom-call | flops 1 | bytes 1 | tf_op jit(solution)/shard_map/pick_rows/pallas_call | solution.py:98
  27.6 3.2 %collective-permute-done.2 = f32[8,128]{1,0:T(8,128)S(1)} collective-permute-done((f32[8,128]{1,0:T(8,128)S(1)}, f32[8,128]{1,0:T(8,128)S(1)}, u32[]{:S(2)}, u32[]{:S(2)}) %collective-permute-start.2) | collective-permute-done | bytes 4128 | tf_op jit(solution)/shard_map/ppermute | solution.py:30
  33.7 7.4 %expand_first.1.refs_9_ = f32[2,384,256]{2,1,0:T(8,128)S(1)} custom-call(s32[1]{0:T(128)} %bitcast.2.refs_2_.refs_0_, bf16[384,768]{1,0:T(8,128)(2,1)S(1)} %get-tuple-element.68.refs_1_, bf16[384,768]{1,0:T(8,128)(2,1)S(1)} %collective-permute-done.3.refs_2_, bf16[384,768]{1,0:T(8,128)(2,1)S(1)} %collective-permute-done.refs_0_.refs_3_, ...), custom_call_target="tpu_custom_call" | custom-call | flops 1 | bytes 1 | tf_op jit(solution)/shard_map/expand_first/pallas_call | solution.py:218
  41.1 7.4 %expand_last.1 = (bf16[192,1024]{1,0:T(8,128)(2,1)S(1)}, bf16[192,1024]{1,0:T(8,128)(2,1)S(1)}) custom-call(s32[1]{0:T(128)} %bitcast.2.refs_2_.refs_0_, bf16[384,768]{1,0:T(8,128)(2,1)S(1)} %get-tuple-element.68.refs_1_, bf16[384,768]{1,0:T(8,128)(2,1)S(1)} %collective-permute-done.3.refs_2_, bf16[384,768]{1,0:T(8,128)(2,1)S(1)} %collective-permute-done.refs_0_.refs_3_, ...), custom_call_target="tpu_custom_call" | custom-call | flops 1 | bytes 1 | tf_op jit(solution)/shard_map/expand_last/pallas_call | solution.py:218
  55.9 10.8 %multiply.1.refs_5_.refs_2_.refs_7_ = f32[2,384,1024]{2,1,0:T(8,128)S(1)} custom-call(s32[1]{0:T(128)} %bitcast.2.refs_2_.refs_0_, bf16[384,768]{1,0:T(8,128)(2,1)S(1)} %get-tuple-element.72.refs_2_.refs_1_, bf16[384,768]{1,0:T(8,128)(2,1)S(1)} %collective-permute-done.11.refs_5_.refs_2_, bf16[384,768]{1,0:T(8,128)(2,1)S(1)} %get-tuple-element.75.refs_3_, ...), custom_call_target="tpu_custom_call" | custom-call | flops 1 | bytes 1 | tf_op jit(solution)/shard_map/multiply/pallas_call | solution.py:327
  67.5 2.3 %collective-permute-done.16.refs_2_ = bf16[192,1024]{1,0:T(8,128)(2,1)S(1)} collective-permute-done((bf16[192,1024]{1,0:T(8,128)(2,1)S(1)}, bf16[192,1024]{1,0:T(8,128)(2,1)S(1)}, u32[]{:S(2)}, u32[]{:S(2)}) %collective-permute-start.16) | collective-permute-done | bytes 393248 | tf_op jit(solution)/shard_map/ppermute | solution.py:30
  72.1 5.1 %multiply_last.1 = (bf16[192,1024]{1,0:T(8,128)(2,1)S(1)}, bf16[192,1024]{1,0:T(8,128)(2,1)S(1)}) custom-call(s32[1]{0:T(128)} %bitcast.2.refs_2_.refs_0_, bf16[128,768]{1,0:T(8,128)(2,1)S(1)} %get-tuple-element.83.refs_1_, bf16[128,768]{1,0:T(8,128)(2,1)S(1)} %get-tuple-element.84.refs_2_, bf16[128,768]{1,0:T(8,128)(2,1)S(1)} %get-tuple-element.85.refs_3_, ...), custom_call_target="tpu_custom_call" | custom-call | flops 1 | bytes 1 | tf_op jit(solution)/shard_map/multiply_last/pallas_call | solution.py:327
  77.8 2.9 %collective-permute-done.18.refs_2_ = bf16[192,1024]{1,0:T(8,128)(2,1)S(1)} collective-permute-done((bf16[192,1024]{1,0:T(8,128)(2,1)S(1)}, bf16[192,1024]{1,0:T(8,128)(2,1)S(1)}, u32[]{:S(2)}, u32[]{:S(2)}) %collective-permute-start.18) | collective-permute-done | bytes 393248 | tf_op jit(solution)/shard_map/ppermute | solution.py:30
  85.0 6.6 %collective-permute-done.27.refs_2_ = bf16[192,1024]{1,0:T(8,128)(2,1)S(1)} collective-permute-done((bf16[192,1024]{1,0:T(8,128)(2,1)S(1)}, bf16[192,1024]{1,0:T(8,128)(2,1)S(1)}, u32[]{:S(2)}, u32[]{:S(2)}) %collective-permute-start.27) | collective-permute-done | bytes 393248 | tf_op jit(solution)/shard_map/ppermute | solution.py:30
  94.9 6.3 %collective-permute-done.29.refs_2_ = bf16[192,1024]{1,0:T(8,128)(2,1)S(1)} collective-permute-done((bf16[192,1024]{1,0:T(8,128)(2,1)S(1)}, bf16[192,1024]{1,0:T(8,128)(2,1)S(1)}, u32[]{:S(2)}, u32[]{:S(2)}) %collective-permute-start.29) | collective-permute-done | bytes 393248 | tf_op jit(solution)/shard_map/ppermute | solution.py:30
  105.7 2.4 %collective-permute-done.32 = f32[16,128]{1,0:T(8,128)S(1)} collective-permute-done((f32[16,128]{1,0:T(8,128)S(1)}, f32[16,128]{1,0:T(8,128)S(1)}, u32[]{:S(2)}, u32[]{:S(2)}) %collective-permute-start.32) | collective-permute-done | bytes 8224 | tf_op jit(solution)/shard_map/ppermute | solution.py:30
  110.3 2.1 %collective-permute-done.34 = f32[16,128]{1,0:T(8,128)S(1)} collective-permute-done((f32[16,128]{1,0:T(8,128)S(1)}, f32[16,128]{1,0:T(8,128)S(1)}, u32[]{:S(2)}, u32[]{:S(2)}) %collective-permute-start.34) | collective-permute-done | bytes 8224 | tf_op jit(solution)/shard_map/ppermute | solution.py:619
  112.4 2.6 %collective-permute-start.35 = (f32[16,128]{1,0:T(8,128)S(1)}, f32[16,128]{1,0:T(8,128)S(1)}, u32[]{:S(2)}, u32[]{:S(2)}) collective-permute-start(f32[16,128]{1,0:T(8,128)S(1)} %fusion), channel_id=1, source_target_pairs={{0,2},{1,3},{2,0},{3,1},{4,6},{5,7},{6,4},{7,5},{8,10},{9,11},{10,... | collective-permute-start | bytes 24584 | tf_op jit(solution)/shard_map/ppermute | solution.py:619
  116.9 5.4 %down.3 = (bf16[768,1024]{1,0:T(8,128)(2,1)S(1)}, bf16[4,768,256]{2,1,0:T(8,128)(2,1)S(1)}, bf16[4,768,256]{2,1,0:T(8,128)(2,1)S(1)}) custom-call(s32[1]{0:T(128)} %bitcast.2.refs_2_.refs_0_, f32[16,128]{1,0:T(8,128)S(1)} %max.39.refs_1_.values_ref, bf16[192,1024]{1,0:T(8,128)(2,1)S(1)} %get-tuple-element.96.refs_2_, ...), custom_call_target="tpu_custom_call" | custom-call | flops 1 | bytes 1 | tf_op jit(solution)/shard_map/down/pallas_call | solution.py:407
  122.5 5.2 %down.4 = (bf16[4,768,256]{2,1,0:T(8,128)(2,1)S(1)}, bf16[4,768,256]{2,1,0:T(8,128)(2,1)S(1)}) custom-call(s32[1]{0:T(128)} %bitcast.2.refs_2_.refs_0_, bf16[768,1024]{1,0:T(8,128)(2,1)S(1)} %get-tuple-element.100.refs_1_, bf16[1024,6144]{1,0:T(8,128)(2,1)} %refs_2_.3, bf16[4,768,256]{2,1,0:T(8,128)(2,1)S(1)} %get-tuple-element.101.refs_3_.refs_0_), custom_call_target="tpu_custom_call" | custom-call | flops 1 | bytes 1 | tf_op jit(solution)/shard_map/down/pallas_call | solution.py:407
  130.6 5.2 %down.5 = (bf16[4,768,256]{2,1,0:T(8,128)(2,1)S(1)}, bf16[4,768,256]{2,1,0:T(8,128)(2,1)S(1)}) custom-call(s32[1]{0:T(128)} %bitcast.2.refs_2_.refs_0_, bf16[768,1024]{1,0:T(8,128)(2,1)S(1)} %get-tuple-element.100.refs_1_, bf16[1024,6144]{1,0:T(8,128)(2,1)} %refs_2_.3, bf16[2,384,256]{2,1,0:T(8,128)(2,1)S(1)} %get-tuple-element.104.refs_3_.refs_0_, ...), custom_call_target="tpu_custom_call" | custom-call | flops 1 | bytes 1 | tf_op jit(solution)/shard_map/down/pallas_call | solution.py:407
  136.2 3.5 %collective-permute-done.37.refs_1_ = bf16[2,384,256]{2,1,0:T(8,128)(2,1)S(1)} collective-permute-done((bf16[2,384,256]{2,1,0:T(8,128)(2,1)S(1)}, bf16[2,384,256]{2,1,0:T(8,128)(2,1)S(1)}, u32[]{:S(2)}, u32[]{:S(2)}) %collective-permute-start.37) | collective-permute-done | bytes 393248 | tf_op jit(solution)/shard_map/ppermute | solution.py:30
  147.1 5.3 %collective-permute-done.43.refs_1_ = bf16[2,384,256]{2,1,0:T(8,128)(2,1)S(1)} collective-permute-done((bf16[2,384,256]{2,1,0:T(8,128)(2,1)S(1)}, bf16[2,384,256]{2,1,0:T(8,128)(2,1)S(1)}, u32[]{:S(2)}, u32[]{:S(2)}) %collective-permute-start.43) | collective-permute-done | bytes 393248 | tf_op jit(solution)/shard_map/ppermute | solution.py:30
  156.1 4.7 %collective-permute-done.41.refs_1_ = bf16[2,384,256]{2,1,0:T(8,128)(2,1)S(1)} collective-permute-done((bf16[2,384,256]{2,1,0:T(8,128)(2,1)S(1)}, bf16[2,384,256]{2,1,0:T(8,128)(2,1)S(1)}, u32[]{:S(2)}, u32[]{:S(2)}) %collective-permute-start.41) | collective-permute-done | bytes 393248 | tf_op jit(solution)/shard_map/ppermute | solution.py:30
  166.3 4.4 %collective-permute-done.47.refs_4_.refs_8_ = bf16[2,384,256]{2,1,0:T(8,128)(2,1)S(1)} collective-permute-done((bf16[2,384,256]{2,1,0:T(8,128)(2,1)S(1)}, bf16[2,384,256]{2,1,0:T(8,128)(2,1)S(1)}, u32[]{:S(2)}, u32[]{:S(2)}) %collective-permute-start.47) | collective-permute-done | bytes 393248 | tf_op jit(solution)/shard_map/ppermute | solution.py:30
  170.7 2.9 %spread.2.refs_6_ = bf16[1536,768]{1,0:T(8,128)(2,1)} custom-call(s32[2,1536]{1,0:T(2,128)S(1)} %bitcast.5, f32[2,1536]{1,0:T(2,128)S(1)} %bitcast.7, bf16[1,384,256]{2,1,0:T(8,128)(2,1)S(1)} %get-tuple-element.114.refs_2_, bf16[1,384,256]{2,1,0:T(8,128)(2,1)S(1)} %get-tuple-element.115.refs_3_, ...), custom_call_target="tpu_custom_call" | custom-call | flops 1 | bytes 1 | tf_op jit(solution)/shard_map/spread/pallas_call | solution.py:465
  (121 shorter events, 57.9 us)
Async XLA Ops:
  3.9 16.4 %collective-permute-start.1 = (bf16[384,768]{1,0:T(8,128)(2,1)S(1)}, bf16[384,768]{1,0:T(8,128)(2,1)S(1)}, u32[]{:S(2)}, u32[]{:S(2)}) collective-permute-start(bf16[384,768]{1,0:T(8,128)(2,1)S(1)} %get-tuple-element.68.refs_1_), channel_id=1, source_target_pairs={{0,16},{4,20},{8,24},{12,28},{16,0},{20,4},{24,8},{28,12},{1,17},{... | collective-permute-start | bytes 1769480 | tf_op jit(solution)/shard_map/ppermute | solution.py:30
  7.0 14.8 %collective-permute-start = (bf16[384,768]{1,0:T(8,128)(2,1)S(1)}, bf16[384,768]{1,0:T(8,128)(2,1)S(1)}, u32[]{:S(2)}, u32[]{:S(2)}) collective-permute-start(bf16[384,768]{1,0:T(8,128)(2,1)S(1)} %get-tuple-element.68.refs_1_), channel_id=1, source_target_pairs={{0,8},{4,12},{8,0},{12,4},{16,24},{20,28},{24,16},{28,20},{1,9},{5... | collective-permute-start | bytes 1769480 | tf_op jit(solution)/shard_map/ppermute | solution.py:30
  8.5 24.5 %collective-permute-start.3 = (bf16[384,768]{1,0:T(8,128)(2,1)S(1)}, bf16[384,768]{1,0:T(8,128)(2,1)S(1)}, u32[]{:S(2)}, u32[]{:S(2)}) collective-permute-start(bf16[384,768]{1,0:T(8,128)(2,1)S(1)} %get-tuple-element.68.refs_1_), channel_id=1, source_target_pairs={{0,4},{4,0},{8,12},{12,8},{16,20},{20,16},{24,28},{28,24},{1,5},{5... | collective-permute-start | bytes 1769480 | tf_op jit(solution)/shard_map/ppermute | solution.py:30
  23.9 9.7 %collective-permute-start.5 = (bf16[384,768]{1,0:T(8,128)(2,1)S(1)}, bf16[384,768]{1,0:T(8,128)(2,1)S(1)}, u32[]{:S(2)}, u32[]{:S(2)}) collective-permute-start(bf16[384,768]{1,0:T(8,128)(2,1)S(1)} %collective-permute-done.1.refs_1_.refs_5_), channel_id=1, source_target_pairs={{0,4},{4,0},{8,12},{12,8},{16,20},{20,16},{24,28},{28,24},{1,5},{5... | collective-permute-start | bytes 1769480 | tf_op jit(solution)/shard_map/ppermute | solution.py:30
  31.5 17.0 %collective-permute-start.13 = (bf16[384,768]{1,0:T(8,128)(2,1)S(1)}, bf16[384,768]{1,0:T(8,128)(2,1)S(1)}, u32[]{:S(2)}, u32[]{:S(2)}) collective-permute-start(bf16[384,768]{1,0:T(8,128)(2,1)S(1)} %get-tuple-element.72.refs_2_.refs_1_), channel_id=1, source_target_pairs={{0,16},{4,20},{8,24},{12,28},{16,0},{20,4},{24,8},{28,12},{1,17},{... | collective-permute-start | bytes 1769480 | tf_op jit(solution)/shard_map/ppermute | solution.py:30
  33.0 15.5 %collective-permute-start.12 = (bf16[384,768]{1,0:T(8,128)(2,1)S(1)}, bf16[384,768]{1,0:T(8,128)(2,1)S(1)}, u32[]{:S(2)}, u32[]{:S(2)}) collective-permute-start(bf16[384,768]{1,0:T(8,128)(2,1)S(1)} %get-tuple-element.72.refs_2_.refs_1_), channel_id=1, source_target_pairs={{0,8},{4,12},{8,0},{12,4},{16,24},{20,28},{24,16},{28,20},{1,9},{5... | collective-permute-start | bytes 1769480 | tf_op jit(solution)/shard_map/ppermute | solution.py:30
  33.5 16.2 %collective-permute-start.11 = (bf16[384,768]{1,0:T(8,128)(2,1)S(1)}, bf16[384,768]{1,0:T(8,128)(2,1)S(1)}, u32[]{:S(2)}, u32[]{:S(2)}) collective-permute-start(bf16[384,768]{1,0:T(8,128)(2,1)S(1)} %get-tuple-element.72.refs_2_.refs_1_), channel_id=1, source_target_pairs={{0,4},{4,0},{8,12},{12,8},{16,20},{20,16},{24,28},{28,24},{1,5},{5... | collective-permute-start | bytes 1769480 | tf_op jit(solution)/shard_map/ppermute | solution.py:30
  49.7 17.1 %collective-permute-start.20 = (bf16[192,768]{1,0:T(8,128)(2,1)S(1)}, bf16[192,768]{1,0:T(8,128)(2,1)S(1)}, u32[]{:S(2)}, u32[]{:S(2)}) collective-permute-start(bf16[192,768]{1,0:T(8,128)(2,1)S(1)} %get-tuple-element.81), channel_id=1, source_target_pairs={{0,16},{4,20},{8,24},{12,28},{16,0},{20,4},{24,8},{28,12},{1,17},{... | collective-permute-start | bytes 884744 | tf_op jit(solution)/shard_map/ppermute | solution.py:30
  52.1 14.7 %collective-permute-start.21 = (bf16[192,768]{1,0:T(8,128)(2,1)S(1)}, bf16[192,768]{1,0:T(8,128)(2,1)S(1)}, u32[]{:S(2)}, u32[]{:S(2)}) collective-permute-start(bf16[192,768]{1,0:T(8,128)(2,1)S(1)} %get-tuple-element.82), channel_id=1, source_target_pairs={{0,8},{4,12},{8,0},{12,4},{16,24},{20,28},{24,16},{28,20},{1,9},{5... | collective-permute-start | bytes 884744 | tf_op jit(solution)/shard_map/ppermute | solution.py:30
  53.8 16.0 %collective-permute-start.16 = (bf16[192,1024]{1,0:T(8,128)(2,1)S(1)}, bf16[192,1024]{1,0:T(8,128)(2,1)S(1)}, u32[]{:S(2)}, u32[]{:S(2)}) collective-permute-start(bf16[192,1024]{1,0:T(8,128)(2,1)S(1)} %get-tuple-element.77.refs_9_.refs_1_), channel_id=1, source_target_pairs={{0,8},{4,12},{8,0},{12,4},{16,24},{20,28},{24,16},{28,20},{1,9},{5... | collective-permute-start | bytes 1179656 | tf_op jit(solution)/shard_map/ppermute | solution.py:30
  54.5 15.3 %collective-permute-start.17 = (bf16[192,1024]{1,0:T(8,128)(2,1)S(1)}, bf16[192,1024]{1,0:T(8,128)(2,1)S(1)}, u32[]{:S(2)}, u32[]{:S(2)}) collective-permute-start(bf16[192,1024]{1,0:T(8,128)(2,1)S(1)} %get-tuple-element.78.refs_10_.refs_3_), channel_id=1, source_target_pairs={{0,16},{4,20},{8,24},{12,28},{16,0},{20,4},{24,8},{28,12},{1,17},{... | collective-permute-start | bytes 1179656 | tf_op jit(solution)/shard_map/ppermute | solution.py:30
  70.0 10.6 %collective-permute-start.18 = (bf16[192,1024]{1,0:T(8,128)(2,1)S(1)}, bf16[192,1024]{1,0:T(8,128)(2,1)S(1)}, u32[]{:S(2)}, u32[]{:S(2)}) collective-permute-start(bf16[192,1024]{1,0:T(8,128)(2,1)S(1)} %get-tuple-element.79.refs_10_.refs_1_), channel_id=1, source_target_pairs={{0,16},{4,20},{8,24},{12,28},{16,0},{20,4},{24,8},{28,12},{1,17},{... | collective-permute-start | bytes 1179656 | tf_op jit(solution)/shard_map/ppermute | solution.py:30
  71.4 10.0 %collective-permute-start.19 = (bf16[192,1024]{1,0:T(8,128)(2,1)S(1)}, bf16[192,1024]{1,0:T(8,128)(2,1)S(1)}, u32[]{:S(2)}, u32[]{:S(2)}) collective-permute-start(bf16[192,1024]{1,0:T(8,128)(2,1)S(1)} %get-tuple-element.80.refs_11_.refs_3_), channel_id=1, source_target_pairs={{0,8},{4,12},{8,0},{12,4},{16,24},{20,28},{24,16},{28,20},{1,9},{5... | collective-permute-start | bytes 1179656 | tf_op jit(solution)/shard_map/ppermute | solution.py:30
  83.4 9.2 %collective-permute-start.28 = (bf16[192,1024]{1,0:T(8,128)(2,1)S(1)}, bf16[192,1024]{1,0:T(8,128)(2,1)S(1)}, u32[]{:S(2)}, u32[]{:S(2)}) collective-permute-start(bf16[192,1024]{1,0:T(8,128)(2,1)S(1)} %get-tuple-element.91.refs_3_), channel_id=1, source_target_pairs={{0,16},{4,20},{8,24},{12,28},{16,0},{20,4},{24,8},{28,12},{1,17},{... | collective-permute-start | bytes 1179656 | tf_op jit(solution)/shard_map/ppermute | solution.py:30
  128.6 11.1 %collective-permute-start.37 = (bf16[2,384,256]{2,1,0:T(8,128)(2,1)S(1)}, bf16[2,384,256]{2,1,0:T(8,128)(2,1)S(1)}, u32[]{:S(2)}, u32[]{:S(2)}) collective-permute-start(bf16[2,384,256]{2,1,0:T(8,128)(2,1)S(1)} %get-tuple-element.107), channel_id=1, source_target_pairs={{0,8},{4,12},{8,0},{12,4},{16,24},{20,28},{24,16},{28,20},{1,9},{5... | collective-permute-start | bytes 1179656 | tf_op jit(solution)/shard_map/ppermute | solution.py:30
  129.2 10.8 %collective-permute-start.38 = (bf16[2,384,256]{2,1,0:T(8,128)(2,1)S(1)}, bf16[2,384,256]{2,1,0:T(8,128)(2,1)S(1)}, u32[]{:S(2)}, u32[]{:S(2)}) collective-permute-start(bf16[2,384,256]{2,1,0:T(8,128)(2,1)S(1)} %get-tuple-element.108), channel_id=1, source_target_pairs={{0,16},{4,20},{8,24},{12,28},{16,0},{20,4},{24,8},{28,12},{1,17},{... | collective-permute-start | bytes 1179656 | tf_op jit(solution)/shard_map/ppermute | solution.py:30
  140.4 12.0 %collective-permute-start.43 = (bf16[2,384,256]{2,1,0:T(8,128)(2,1)S(1)}, bf16[2,384,256]{2,1,0:T(8,128)(2,1)S(1)}, u32[]{:S(2)}, u32[]{:S(2)}) collective-permute-start(bf16[2,384,256]{2,1,0:T(8,128)(2,1)S(1)} %get-tuple-element.120), channel_id=1, source_target_pairs={{0,8},{4,12},{8,0},{12,4},{16,24},{20,28},{24,16},{28,20},{1,9},{5... | collective-permute-start | bytes 1179656 | tf_op jit(solution)/shard_map/ppermute | solution.py:30
  141.9 12.0 %collective-permute-start.44 = (bf16[2,384,256]{2,1,0:T(8,128)(2,1)S(1)}, bf16[2,384,256]{2,1,0:T(8,128)(2,1)S(1)}, u32[]{:S(2)}, u32[]{:S(2)}) collective-permute-start(bf16[2,384,256]{2,1,0:T(8,128)(2,1)S(1)} %get-tuple-element.121), channel_id=1, source_target_pairs={{0,16},{4,20},{8,24},{12,28},{16,0},{20,4},{24,8},{28,12},{1,17},{... | collective-permute-start | bytes 1179656 | tf_op jit(solution)/shard_map/ppermute | solution.py:30
  144.2 16.6 %collective-permute-start.41 = (bf16[2,384,256]{2,1,0:T(8,128)(2,1)S(1)}, bf16[2,384,256]{2,1,0:T(8,128)(2,1)S(1)}, u32[]{:S(2)}, u32[]{:S(2)}) collective-permute-start(bf16[2,384,256]{2,1,0:T(8,128)(2,1)S(1)} %get-tuple-element.117), channel_id=1, source_target_pairs={{0,8},{4,12},{8,0},{12,4},{16,24},{20,28},{24,16},{28,20},{1,9},{5... | collective-permute-start | bytes 1179656 | tf_op jit(solution)/shard_map/ppermute | solution.py:30
  145.7 16.6 %collective-permute-start.42 = (bf16[2,384,256]{2,1,0:T(8,128)(2,1)S(1)}, bf16[2,384,256]{2,1,0:T(8,128)(2,1)S(1)}, u32[]{:S(2)}, u32[]{:S(2)}) collective-permute-start(bf16[2,384,256]{2,1,0:T(8,128)(2,1)S(1)} %get-tuple-element.119), channel_id=1, source_target_pairs={{0,16},{4,20},{8,24},{12,28},{16,0},{20,4},{24,8},{28,12},{1,17},{... | collective-permute-start | bytes 1179656 | tf_op jit(solution)/shard_map/ppermute | solution.py:30
  154.1 16.6 %collective-permute-start.47 = (bf16[2,384,256]{2,1,0:T(8,128)(2,1)S(1)}, bf16[2,384,256]{2,1,0:T(8,128)(2,1)S(1)}, u32[]{:S(2)}, u32[]{:S(2)}) collective-permute-start(bf16[2,384,256]{2,1,0:T(8,128)(2,1)S(1)} %get-tuple-element.130), channel_id=1, source_target_pairs={{0,16},{4,20},{8,24},{12,28},{16,0},{20,4},{24,8},{28,12},{1,17},{... | collective-permute-start | bytes 1179656 | tf_op jit(solution)/shard_map/ppermute | solution.py:30
  155.5 15.2 %collective-permute-start.48 = (bf16[2,384,256]{2,1,0:T(8,128)(2,1)S(1)}, bf16[2,384,256]{2,1,0:T(8,128)(2,1)S(1)}, u32[]{:S(2)}, u32[]{:S(2)}) collective-permute-start(bf16[2,384,256]{2,1,0:T(8,128)(2,1)S(1)} %get-tuple-element.131), channel_id=1, source_target_pairs={{0,8},{4,12},{8,0},{12,4},{16,24},{20,28},{24,16},{28,20},{1,9},{5... | collective-permute-start | bytes 1179656 | tf_op jit(solution)/shard_map/ppermute | solution.py:30
  163.1 11.1 %collective-permute-start.45 = (bf16[1,384,256]{2,1,0:T(8,128)(2,1)}, bf16[1,384,256]{2,1,0:T(8,128)(2,1)S(1)}, u32[]{:S(2)}, u32[]{:S(2)}) collective-permute-start(bf16[1,384,256]{2,1,0:T(8,128)(2,1)} %get-tuple-element.128), channel_id=1, source_target_pairs={{0,16},{4,20},{8,24},{12,28},{16,0},{20,4},{24,8},{28,12},{1,17},{... | collective-permute-start | bytes 589832 | tf_op jit(solution)/shard_map/ppermute | solution.py:30
  164.4 9.7 %collective-permute-start.46 = (bf16[1,384,256]{2,1,0:T(8,128)(2,1)S(1)}, bf16[1,384,256]{2,1,0:T(8,128)(2,1)S(1)}, u32[]{:S(2)}, u32[]{:S(2)}) collective-permute-start(bf16[1,384,256]{2,1,0:T(8,128)(2,1)S(1)} %get-tuple-element.129), channel_id=1, source_target_pairs={{0,8},{4,12},{8,0},{12,4},{16,24},{20,28},{24,16},{28,20},{1,9},{5... | collective-permute-start | bytes 589832 | tf_op jit(solution)/shard_map/ppermute | solution.py:30
  (28 other events, 166.8 us)

commit v2 on v1

--- a/solution.py
+++ b/solution.py
@@ -15,7 +15,7 @@
 F32 = jnp.float32
 MIB = 1 << 20
 EXPAND_MIB = 24
-AHEAD = 3
+AHEAD = 2
 
 
 def params(mib):

time: 177 us -> 176 us (level)
  no operation moved by 1% of the time
where the time goes in v2:
time: 176 us
  waiting for transfers between devices  69 us (39%)
  Pallas kernels  64.5 us (37%)
  starting transfers between devices  41.6 us (24%)
    ppermute x47, waiting for transfers between devices, across(): lax.ppermute(block, 'tensor', [(r, r ^ 1 << bit) for r in range(count)])  65 us
    ppermute x47, starting transfers between devices, across(): lax.ppermute(block, 'tensor', [(r, r ^ 1 << bit) for r in range(count)])  37.5 us
    pallas_call x2, Pallas kernels, multiply(): pl.pallas_call(lambda *refs: multiply_body(masks, cuts, resumed, last, *r...  15.9 us
    pallas_call x3, Pallas kernels, down(): pl.pallas_call(lambda *refs: down_body(first * LANES, len(fresh), *refs),...  15.9 us
    pallas_call x2, Pallas kernels, expand(): pl.pallas_call(lambda *refs: expand_body(first, cuts, last, *refs[:used],...  14.8 us
    pallas_call x2, Pallas kernels, pick_rows(): pl.pallas_call(lambda *refs: pick_body(first, *refs), out_shape=(jax.Shap...  6.56 us
    pallas_call x16, Pallas kernels, small(): pl.pallas_call(lambda *refs: body(refs[:count], refs[count + len(follow):...  5.06 us
    pallas_call x2, Pallas kernels, spread(): pl.pallas_call(lambda *refs: spread_body(counts, slots_at, *refs[:used],...  4.97 us
  transfers between devices with their start and end apart: 49, of which 26 were waited for; matrix products, arithmetic and copies ran while one was open for 0% of the time, Pallas kernels for 30%

profile of v2, /device:TPU:0, one launch (start us, length us, event | category | flops | bytes accessed | tf_op | source)
XLA Modules:
  0.0 176.2 jit_solution(13175072946352575494)
XLA Ops:
  0.6 3.3 %pick_rows.2 = (bf16[384,768]{1,0:T(8,128)(2,1)S(1)}, f32[8,128]{1,0:T(8,128)S(1)}) custom-call(s32[2,1536]{1,0:T(2,128)} %bitcast.3, bf16[1536,768]{1,0:T(8,128)(2,1)} %refs_1_.3, s32[1]{0:T(128)} %bitcast.2.refs_2_.refs_0_), custom_call_target="tpu_custom_call" | custom-call | flops 1 | bytes 1 | tf_op jit(solution)/shard_map/pick_rows/pallas_call | solution.py:98
  3.9 3.0 %collective-permute-start.1 = (bf16[384,768]{1,0:T(8,128)(2,1)S(1)}, bf16[384,768]{1,0:T(8,128)(2,1)S(1)}, u32[]{:S(2)}, u32[]{:S(2)}) collective-permute-start(bf16[384,768]{1,0:T(8,128)(2,1)S(1)} %get-tuple-element.68.refs_1_), channel_id=1, source_target_pairs={{0,16},{4,20},{8,24},{12,28},{16,0},{20,4},{24,8},{28,12},{1,17},{... | collective-permute-start | bytes 1769480 | tf_op jit(solution)/shard_map/ppermute | solution.py:30
  8.5 11.8 %collective-permute-done.1.refs_1_.refs_5_ = bf16[384,768]{1,0:T(8,128)(2,1)S(1)} collective-permute-done((bf16[384,768]{1,0:T(8,128)(2,1)S(1)}, bf16[384,768]{1,0:T(8,128)(2,1)S(1)}, u32[]{:S(2)}, u32[]{:S(2)}) %collective-permute-start.1) | collective-permute-done | bytes 589856 | tf_op jit(solution)/shard_map/ppermute | solution.py:30
  23.9 3.3 %pick_rows.3 = (bf16[384,768]{1,0:T(8,128)(2,1)S(1)}, f32[8,128]{1,0:T(8,128)S(1)}) custom-call(s32[2,1536]{1,0:T(2,128)} %bitcast.4, bf16[1536,768]{1,0:T(8,128)(2,1)} %refs_1_.3, bf16[192,768]{1,0:T(8,128)(2,1)S(1)} %get-tuple-element.69.refs_2_, bf16[192,768]{1,0:T(8,128)(2,1)S(1)} %get-tuple-element.70.refs_3_), custom_call_target="tpu_custom_call" | custom-call | flops 1 | bytes 1 | tf_op jit(solution)/shard_map/pick_rows/pallas_call | solution.py:98
  27.6 3.2 %collective-permute-done.2 = f32[8,128]{1,0:T(8,128)S(1)} collective-permute-done((f32[8,128]{1,0:T(8,128)S(1)}, f32[8,128]{1,0:T(8,128)S(1)}, u32[]{:S(2)}, u32[]{:S(2)}) %collective-permute-start.2) | collective-permute-done | bytes 4128 | tf_op jit(solution)/shard_map/ppermute | solution.py:30
  33.7 7.4 %expand_first.1.refs_9_ = f32[2,384,256]{2,1,0:T(8,128)S(1)} custom-call(s32[1]{0:T(128)} %bitcast.2.refs_2_.refs_0_, bf16[384,768]{1,0:T(8,128)(2,1)S(1)} %get-tuple-element.68.refs_1_, bf16[384,768]{1,0:T(8,128)(2,1)S(1)} %collective-permute-done.3.refs_2_, bf16[384,768]{1,0:T(8,128)(2,1)S(1)} %collective-permute-done.refs_0_.refs_3_, ...), custom_call_target="tpu_custom_call" | custom-call | flops 1 | bytes 1 | tf_op jit(solution)/shard_map/expand_first/pallas_call | solution.py:218
  41.1 7.4 %expand_last.1 = (bf16[192,1024]{1,0:T(8,128)(2,1)S(1)}, bf16[192,1024]{1,0:T(8,128)(2,1)S(1)}) custom-call(s32[1]{0:T(128)} %bitcast.2.refs_2_.refs_0_, bf16[384,768]{1,0:T(8,128)(2,1)S(1)} %get-tuple-element.68.refs_1_, bf16[384,768]{1,0:T(8,128)(2,1)S(1)} %collective-permute-done.3.refs_2_, bf16[384,768]{1,0:T(8,128)(2,1)S(1)} %collective-permute-done.refs_0_.refs_3_, ...), custom_call_target="tpu_custom_call" | custom-call | flops 1 | bytes 1 | tf_op jit(solution)/shard_map/expand_last/pallas_call | solution.py:218
  55.9 10.8 %multiply.1.refs_5_.refs_2_.refs_7_ = f32[2,384,1024]{2,1,0:T(8,128)S(1)} custom-call(s32[1]{0:T(128)} %bitcast.2.refs_2_.refs_0_, bf16[384,768]{1,0:T(8,128)(2,1)S(1)} %get-tuple-element.72.refs_2_.refs_1_, bf16[384,768]{1,0:T(8,128)(2,1)S(1)} %collective-permute-done.11.refs_5_.refs_2_, bf16[384,768]{1,0:T(8,128)(2,1)S(1)} %get-tuple-element.75.refs_3_, ...), custom_call_target="tpu_custom_call" | custom-call | flops 1 | bytes 1 | tf_op jit(solution)/shard_map/multiply/pallas_call | solution.py:327
  67.5 2.3 %collective-permute-done.16.refs_2_ = bf16[192,1024]{1,0:T(8,128)(2,1)S(1)} collective-permute-done((bf16[192,1024]{1,0:T(8,128)(2,1)S(1)}, bf16[192,1024]{1,0:T(8,128)(2,1)S(1)}, u32[]{:S(2)}, u32[]{:S(2)}) %collective-permute-start.16) | collective-permute-done | bytes 393248 | tf_op jit(solution)/shard_map/ppermute | solution.py:30
  72.1 5.1 %multiply_last.1 = (bf16[192,1024]{1,0:T(8,128)(2,1)S(1)}, bf16[192,1024]{1,0:T(8,128)(2,1)S(1)}) custom-call(s32[1]{0:T(128)} %bitcast.2.refs_2_.refs_0_, bf16[128,768]{1,0:T(8,128)(2,1)S(1)} %get-tuple-element.83.refs_1_, bf16[128,768]{1,0:T(8,128)(2,1)S(1)} %get-tuple-element.84.refs_2_, bf16[128,768]{1,0:T(8,128)(2,1)S(1)} %get-tuple-element.85.refs_3_, ...), custom_call_target="tpu_custom_call" | custom-call | flops 1 | bytes 1 | tf_op jit(solution)/shard_map/multiply_last/pallas_call | solution.py:327
  77.8 2.9 %collective-permute-done.18.refs_2_ = bf16[192,1024]{1,0:T(8,128)(2,1)S(1)} collective-permute-done((bf16[192,1024]{1,0:T(8,128)(2,1)S(1)}, bf16[192,1024]{1,0:T(8,128)(2,1)S(1)}, u32[]{:S(2)}, u32[]{:S(2)}) %collective-permute-start.18) | collective-permute-done | bytes 393248 | tf_op jit(solution)/shard_map/ppermute | solution.py:30
  85.0 6.6 %collective-permute-done.27.refs_2_ = bf16[192,1024]{1,0:T(8,128)(2,1)S(1)} collective-permute-done((bf16[192,1024]{1,0:T(8,128)(2,1)S(1)}, bf16[192,1024]{1,0:T(8,128)(2,1)S(1)}, u32[]{:S(2)}, u32[]{:S(2)}) %collective-permute-start.27) | collective-permute-done | bytes 393248 | tf_op jit(solution)/shard_map/ppermute | solution.py:30
  94.9 6.3 %collective-permute-done.29.refs_2_ = bf16[192,1024]{1,0:T(8,128)(2,1)S(1)} collective-permute-done((bf16[192,1024]{1,0:T(8,128)(2,1)S(1)}, bf16[192,1024]{1,0:T(8,128)(2,1)S(1)}, u32[]{:S(2)}, u32[]{:S(2)}) %collective-permute-start.29) | collective-permute-done | bytes 393248 | tf_op jit(solution)/shard_map/ppermute | solution.py:30
  105.7 2.4 %collective-permute-done.32 = f32[16,128]{1,0:T(8,128)S(1)} collective-permute-done((f32[16,128]{1,0:T(8,128)S(1)}, f32[16,128]{1,0:T(8,128)S(1)}, u32[]{:S(2)}, u32[]{:S(2)}) %collective-permute-start.32) | collective-permute-done | bytes 8224 | tf_op jit(solution)/shard_map/ppermute | solution.py:30
  110.3 2.1 %collective-permute-done.34 = f32[16,128]{1,0:T(8,128)S(1)} collective-permute-done((f32[16,128]{1,0:T(8,128)S(1)}, f32[16,128]{1,0:T(8,128)S(1)}, u32[]{:S(2)}, u32[]{:S(2)}) %collective-permute-start.34) | collective-permute-done | bytes 8224 | tf_op jit(solution)/shard_map/ppermute | solution.py:619
  112.4 2.6 %collective-permute-start.35 = (f32[16,128]{1,0:T(8,128)S(1)}, f32[16,128]{1,0:T(8,128)S(1)}, u32[]{:S(2)}, u32[]{:S(2)}) collective-permute-start(f32[16,128]{1,0:T(8,128)S(1)} %fusion), channel_id=1, source_target_pairs={{0,2},{1,3},{2,0},{3,1},{4,6},{5,7},{6,4},{7,5},{8,10},{9,11},{10,... | collective-permute-start | bytes 24584 | tf_op jit(solution)/shard_map/ppermute | solution.py:619
  116.9 5.4 %down.3 = (bf16[768,1024]{1,0:T(8,128)(2,1)S(1)}, bf16[4,768,256]{2,1,0:T(8,128)(2,1)S(1)}, bf16[4,768,256]{2,1,0:T(8,128)(2,1)S(1)}) custom-call(s32[1]{0:T(128)} %bitcast.2.refs_2_.refs_0_, f32[16,128]{1,0:T(8,128)S(1)} %max.39.refs_1_.values_ref, bf16[192,1024]{1,0:T(8,128)(2,1)S(1)} %get-tuple-element.96.refs_2_, ...), custom_call_target="tpu_custom_call" | custom-call | flops 1 | bytes 1 | tf_op jit(solution)/shard_map/down/pallas_call | solution.py:407
  122.5 5.2 %down.4 = (bf16[4,768,256]{2,1,0:T(8,128)(2,1)S(1)}, bf16[4,768,256]{2,1,0:T(8,128)(2,1)S(1)}) custom-call(s32[1]{0:T(128)} %bitcast.2.refs_2_.refs_0_, bf16[768,1024]{1,0:T(8,128)(2,1)S(1)} %get-tuple-element.100.refs_1_, bf16[1024,6144]{1,0:T(8,128)(2,1)} %refs_2_.3, bf16[4,768,256]{2,1,0:T(8,128)(2,1)S(1)} %get-tuple-element.101.refs_3_.refs_0_), custom_call_target="tpu_custom_call" | custom-call | flops 1 | bytes 1 | tf_op jit(solution)/shard_map/down/pallas_call | solution.py:407
  130.6 5.2 %down.5 = (bf16[4,768,256]{2,1,0:T(8,128)(2,1)S(1)}, bf16[4,768,256]{2,1,0:T(8,128)(2,1)S(1)}) custom-call(s32[1]{0:T(128)} %bitcast.2.refs_2_.refs_0_, bf16[768,1024]{1,0:T(8,128)(2,1)S(1)} %get-tuple-element.100.refs_1_, bf16[1024,6144]{1,0:T(8,128)(2,1)} %refs_2_.3, bf16[2,384,256]{2,1,0:T(8,128)(2,1)S(1)} %get-tuple-element.104.refs_3_.refs_0_, ...), custom_call_target="tpu_custom_call" | custom-call | flops 1 | bytes 1 | tf_op jit(solution)/shard_map/down/pallas_call | solution.py:407
  136.2 3.5 %collective-permute-done.37.refs_1_ = bf16[2,384,256]{2,1,0:T(8,128)(2,1)S(1)} collective-permute-done((bf16[2,384,256]{2,1,0:T(8,128)(2,1)S(1)}, bf16[2,384,256]{2,1,0:T(8,128)(2,1)S(1)}, u32[]{:S(2)}, u32[]{:S(2)}) %collective-permute-start.37) | collective-permute-done | bytes 393248 | tf_op jit(solution)/shard_map/ppermute | solution.py:30
  147.1 5.3 %collective-permute-done.43.refs_1_ = bf16[2,384,256]{2,1,0:T(8,128)(2,1)S(1)} collective-permute-done((bf16[2,384,256]{2,1,0:T(8,128)(2,1)S(1)}, bf16[2,384,256]{2,1,0:T(8,128)(2,1)S(1)}, u32[]{:S(2)}, u32[]{:S(2)}) %collective-permute-start.43) | collective-permute-done | bytes 393248 | tf_op jit(solution)/shard_map/ppermute | solution.py:30
  156.1 4.7 %collective-permute-done.41.refs_1_ = bf16[2,384,256]{2,1,0:T(8,128)(2,1)S(1)} collective-permute-done((bf16[2,384,256]{2,1,0:T(8,128)(2,1)S(1)}, bf16[2,384,256]{2,1,0:T(8,128)(2,1)S(1)}, u32[]{:S(2)}, u32[]{:S(2)}) %collective-permute-start.41) | collective-permute-done | bytes 393248 | tf_op jit(solution)/shard_map/ppermute | solution.py:30
  166.3 4.4 %collective-permute-done.47.refs_4_.refs_8_ = bf16[2,384,256]{2,1,0:T(8,128)(2,1)S(1)} collective-permute-done((bf16[2,384,256]{2,1,0:T(8,128)(2,1)S(1)}, bf16[2,384,256]{2,1,0:T(8,128)(2,1)S(1)}, u32[]{:S(2)}, u32[]{:S(2)}) %collective-permute-start.47) | collective-permute-done | bytes 393248 | tf_op jit(solution)/shard_map/ppermute | solution.py:30
  170.7 2.9 %spread.2.refs_6_ = bf16[1536,768]{1,0:T(8,128)(2,1)} custom-call(s32[2,1536]{1,0:T(2,128)S(1)} %bitcast.5, f32[2,1536]{1,0:T(2,128)S(1)} %bitcast.7, bf16[1,384,256]{2,1,0:T(8,128)(2,1)S(1)} %get-tuple-element.114.refs_2_, bf16[1,384,256]{2,1,0:T(8,128)(2,1)S(1)} %get-tuple-element.115.refs_3_, ...), custom_call_target="tpu_custom_call" | custom-call | flops 1 | bytes 1 | tf_op jit(solution)/shard_map/spread/pallas_call | solution.py:465
  (121 shorter events, 57.9 us)
Async XLA Ops:
  3.9 16.4 %collective-permute-start.1 = (bf16[384,768]{1,0:T(8,128)(2,1)S(1)}, bf16[384,768]{1,0:T(8,128)(2,1)S(1)}, u32[]{:S(2)}, u32[]{:S(2)}) collective-permute-start(bf16[384,768]{1,0:T(8,128)(2,1)S(1)} %get-tuple-element.68.refs_1_), channel_id=1, source_target_pairs={{0,16},{4,20},{8,24},{12,28},{16,0},{20,4},{24,8},{28,12},{1,17},{... | collective-permute-start | bytes 1769480 | tf_op jit(solution)/shard_map/ppermute | solution.py:30
  7.0 14.8 %collective-permute-start = (bf16[384,768]{1,0:T(8,128)(2,1)S(1)}, bf16[384,768]{1,0:T(8,128)(2,1)S(1)}, u32[]{:S(2)}, u32[]{:S(2)}) collective-permute-start(bf16[384,768]{1,0:T(8,128)(2,1)S(1)} %get-tuple-element.68.refs_1_), channel_id=1, source_target_pairs={{0,8},{4,12},{8,0},{12,4},{16,24},{20,28},{24,16},{28,20},{1,9},{5... | collective-permute-start | bytes 1769480 | tf_op jit(solution)/shard_map/ppermute | solution.py:30
  8.5 24.5 %collective-permute-start.3 = (bf16[384,768]{1,0:T(8,128)(2,1)S(1)}, bf16[384,768]{1,0:T(8,128)(2,1)S(1)}, u32[]{:S(2)}, u32[]{:S(2)}) collective-permute-start(bf16[384,768]{1,0:T(8,128)(2,1)S(1)} %get-tuple-element.68.refs_1_), channel_id=1, source_target_pairs={{0,4},{4,0},{8,12},{12,8},{16,20},{20,16},{24,28},{28,24},{1,5},{5... | collective-permute-start | bytes 1769480 | tf_op jit(solution)/shard_map/ppermute | solution.py:30
  23.9 9.7 %collective-permute-start.5 = (bf16[384,768]{1,0:T(8,128)(2,1)S(1)}, bf16[384,768]{1,0:T(8,128)(2,1)S(1)}, u32[]{:S(2)}, u32[]{:S(2)}) collective-permute-start(bf16[384,768]{1,0:T(8,128)(2,1)S(1)} %collective-permute-done.1.refs_1_.refs_5_), channel_id=1, source_target_pairs={{0,4},{4,0},{8,12},{12,8},{16,20},{20,16},{24,28},{28,24},{1,5},{5... | collective-permute-start | bytes 1769480 | tf_op jit(solution)/shard_map/ppermute | solution.py:30
  31.5 17.0 %collective-permute-start.13 = (bf16[384,768]{1,0:T(8,128)(2,1)S(1)}, bf16[384,768]{1,0:T(8,128)(2,1)S(1)}, u32[]{:S(2)}, u32[]{:S(2)}) collective-permute-start(bf16[384,768]{1,0:T(8,128)(2,1)S(1)} %get-tuple-element.72.refs_2_.refs_1_), channel_id=1, source_target_pairs={{0,16},{4,20},{8,24},{12,28},{16,0},{20,4},{24,8},{28,12},{1,17},{... | collective-permute-start | bytes 1769480 | tf_op jit(solution)/shard_map/ppermute | solution.py:30
  33.0 15.5 %collective-permute-start.12 = (bf16[384,768]{1,0:T(8,128)(2,1)S(1)}, bf16[384,768]{1,0:T(8,128)(2,1)S(1)}, u32[]{:S(2)}, u32[]{:S(2)}) collective-permute-start(bf16[384,768]{1,0:T(8,128)(2,1)S(1)} %get-tuple-element.72.refs_2_.refs_1_), channel_id=1, source_target_pairs={{0,8},{4,12},{8,0},{12,4},{16,24},{20,28},{24,16},{28,20},{1,9},{5... | collective-permute-start | bytes 1769480 | tf_op jit(solution)/shard_map/ppermute | solution.py:30
  33.5 16.2 %collective-permute-start.11 = (bf16[384,768]{1,0:T(8,128)(2,1)S(1)}, bf16[384,768]{1,0:T(8,128)(2,1)S(1)}, u32[]{:S(2)}, u32[]{:S(2)}) collective-permute-start(bf16[384,768]{1,0:T(8,128)(2,1)S(1)} %get-tuple-element.72.refs_2_.refs_1_), channel_id=1, source_target_pairs={{0,4},{4,0},{8,12},{12,8},{16,20},{20,16},{24,28},{28,24},{1,5},{5... | collective-permute-start | bytes 1769480 | tf_op jit(solution)/shard_map/ppermute | solution.py:30
  49.7 17.1 %collective-permute-start.20 = (bf16[192,768]{1,0:T(8,128)(2,1)S(1)}, bf16[192,768]{1,0:T(8,128)(2,1)S(1)}, u32[]{:S(2)}, u32[]{:S(2)}) collective-permute-start(bf16[192,768]{1,0:T(8,128)(2,1)S(1)} %get-tuple-element.81), channel_id=1, source_target_pairs={{0,16},{4,20},{8,24},{12,28},{16,0},{20,4},{24,8},{28,12},{1,17},{... | collective-permute-start | bytes 884744 | tf_op jit(solution)/shard_map/ppermute | solution.py:30
  52.1 14.7 %collective-permute-start.21 = (bf16[192,768]{1,0:T(8,128)(2,1)S(1)}, bf16[192,768]{1,0:T(8,128)(2,1)S(1)}, u32[]{:S(2)}, u32[]{:S(2)}) collective-permute-start(bf16[192,768]{1,0:T(8,128)(2,1)S(1)} %get-tuple-element.82), channel_id=1, source_target_pairs={{0,8},{4,12},{8,0},{12,4},{16,24},{20,28},{24,16},{28,20},{1,9},{5... | collective-permute-start | bytes 884744 | tf_op jit(solution)/shard_map/ppermute | solution.py:30
  53.8 16.0 %collective-permute-start.16 = (bf16[192,1024]{1,0:T(8,128)(2,1)S(1)}, bf16[192,1024]{1,0:T(8,128)(2,1)S(1)}, u32[]{:S(2)}, u32[]{:S(2)}) collective-permute-start(bf16[192,1024]{1,0:T(8,128)(2,1)S(1)} %get-tuple-element.77.refs_9_.refs_1_), channel_id=1, source_target_pairs={{0,8},{4,12},{8,0},{12,4},{16,24},{20,28},{24,16},{28,20},{1,9},{5... | collective-permute-start | bytes 1179656 | tf_op jit(solution)/shard_map/ppermute | solution.py:30
  54.5 15.3 %collective-permute-start.17 = (bf16[192,1024]{1,0:T(8,128)(2,1)S(1)}, bf16[192,1024]{1,0:T(8,128)(2,1)S(1)}, u32[]{:S(2)}, u32[]{:S(2)}) collective-permute-start(bf16[192,1024]{1,0:T(8,128)(2,1)S(1)} %get-tuple-element.78.refs_10_.refs_3_), channel_id=1, source_target_pairs={{0,16},{4,20},{8,24},{12,28},{16,0},{20,4},{24,8},{28,12},{1,17},{... | collective-permute-start | bytes 1179656 | tf_op jit(solution)/shard_map/ppermute | solution.py:30
  70.0 10.6 %collective-permute-start.18 = (bf16[192,1024]{1,0:T(8,128)(2,1)S(1)}, bf16[192,1024]{1,0:T(8,128)(2,1)S(1)}, u32[]{:S(2)}, u32[]{:S(2)}) collective-permute-start(bf16[192,1024]{1,0:T(8,128)(2,1)S(1)} %get-tuple-element.79.refs_10_.refs_1_), channel_id=1, source_target_pairs={{0,16},{4,20},{8,24},{12,28},{16,0},{20,4},{24,8},{28,12},{1,17},{... | collective-permute-start | bytes 1179656 | tf_op jit(solution)/shard_map/ppermute | solution.py:30
  71.4 10.0 %collective-permute-start.19 = (bf16[192,1024]{1,0:T(8,128)(2,1)S(1)}, bf16[192,1024]{1,0:T(8,128)(2,1)S(1)}, u32[]{:S(2)}, u32[]{:S(2)}) collective-permute-start(bf16[192,1024]{1,0:T(8,128)(2,1)S(1)} %get-tuple-element.80.refs_11_.refs_3_), channel_id=1, source_target_pairs={{0,8},{4,12},{8,0},{12,4},{16,24},{20,28},{24,16},{28,20},{1,9},{5... | collective-permute-start | bytes 1179656 | tf_op jit(solution)/shard_map/ppermute | solution.py:30
  83.4 9.2 %collective-permute-start.28 = (bf16[192,1024]{1,0:T(8,128)(2,1)S(1)}, bf16[192,1024]{1,0:T(8,128)(2,1)S(1)}, u32[]{:S(2)}, u32[]{:S(2)}) collective-permute-start(bf16[192,1024]{1,0:T(8,128)(2,1)S(1)} %get-tuple-element.91.refs_3_), channel_id=1, source_target_pairs={{0,16},{4,20},{8,24},{12,28},{16,0},{20,4},{24,8},{28,12},{1,17},{... | collective-permute-start | bytes 1179656 | tf_op jit(solution)/shard_map/ppermute | solution.py:30
  128.6 11.1 %collective-permute-start.37 = (bf16[2,384,256]{2,1,0:T(8,128)(2,1)S(1)}, bf16[2,384,256]{2,1,0:T(8,128)(2,1)S(1)}, u32[]{:S(2)}, u32[]{:S(2)}) collective-permute-start(bf16[2,384,256]{2,1,0:T(8,128)(2,1)S(1)} %get-tuple-element.107), channel_id=1, source_target_pairs={{0,8},{4,12},{8,0},{12,4},{16,24},{20,28},{24,16},{28,20},{1,9},{5... | collective-permute-start | bytes 1179656 | tf_op jit(solution)/shard_map/ppermute | solution.py:30
  129.2 10.8 %collective-permute-start.38 = (bf16[2,384,256]{2,1,0:T(8,128)(2,1)S(1)}, bf16[2,384,256]{2,1,0:T(8,128)(2,1)S(1)}, u32[]{:S(2)}, u32[]{:S(2)}) collective-permute-start(bf16[2,384,256]{2,1,0:T(8,128)(2,1)S(1)} %get-tuple-element.108), channel_id=1, source_target_pairs={{0,16},{4,20},{8,24},{12,28},{16,0},{20,4},{24,8},{28,12},{1,17},{... | collective-permute-start | bytes 1179656 | tf_op jit(solution)/shard_map/ppermute | solution.py:30
  140.4 12.0 %collective-permute-start.43 = (bf16[2,384,256]{2,1,0:T(8,128)(2,1)S(1)}, bf16[2,384,256]{2,1,0:T(8,128)(2,1)S(1)}, u32[]{:S(2)}, u32[]{:S(2)}) collective-permute-start(bf16[2,384,256]{2,1,0:T(8,128)(2,1)S(1)} %get-tuple-element.120), channel_id=1, source_target_pairs={{0,8},{4,12},{8,0},{12,4},{16,24},{20,28},{24,16},{28,20},{1,9},{5... | collective-permute-start | bytes 1179656 | tf_op jit(solution)/shard_map/ppermute | solution.py:30
  141.9 12.0 %collective-permute-start.44 = (bf16[2,384,256]{2,1,0:T(8,128)(2,1)S(1)}, bf16[2,384,256]{2,1,0:T(8,128)(2,1)S(1)}, u32[]{:S(2)}, u32[]{:S(2)}) collective-permute-start(bf16[2,384,256]{2,1,0:T(8,128)(2,1)S(1)} %get-tuple-element.121), channel_id=1, source_target_pairs={{0,16},{4,20},{8,24},{12,28},{16,0},{20,4},{24,8},{28,12},{1,17},{... | collective-permute-start | bytes 1179656 | tf_op jit(solution)/shard_map/ppermute | solution.py:30
  144.2 16.6 %collective-permute-start.41 = (bf16[2,384,256]{2,1,0:T(8,128)(2,1)S(1)}, bf16[2,384,256]{2,1,0:T(8,128)(2,1)S(1)}, u32[]{:S(2)}, u32[]{:S(2)}) collective-permute-start(bf16[2,384,256]{2,1,0:T(8,128)(2,1)S(1)} %get-tuple-element.117), channel_id=1, source_target_pairs={{0,8},{4,12},{8,0},{12,4},{16,24},{20,28},{24,16},{28,20},{1,9},{5... | collective-permute-start | bytes 1179656 | tf_op jit(solution)/shard_map/ppermute | solution.py:30
  145.7 16.6 %collective-permute-start.42 = (bf16[2,384,256]{2,1,0:T(8,128)(2,1)S(1)}, bf16[2,384,256]{2,1,0:T(8,128)(2,1)S(1)}, u32[]{:S(2)}, u32[]{:S(2)}) collective-permute-start(bf16[2,384,256]{2,1,0:T(8,128)(2,1)S(1)} %get-tuple-element.119), channel_id=1, source_target_pairs={{0,16},{4,20},{8,24},{12,28},{16,0},{20,4},{24,8},{28,12},{1,17},{... | collective-permute-start | bytes 1179656 | tf_op jit(solution)/shard_map/ppermute | solution.py:30
  154.1 16.6 %collective-permute-start.47 = (bf16[2,384,256]{2,1,0:T(8,128)(2,1)S(1)}, bf16[2,384,256]{2,1,0:T(8,128)(2,1)S(1)}, u32[]{:S(2)}, u32[]{:S(2)}) collective-permute-start(bf16[2,384,256]{2,1,0:T(8,128)(2,1)S(1)} %get-tuple-element.130), channel_id=1, source_target_pairs={{0,16},{4,20},{8,24},{12,28},{16,0},{20,4},{24,8},{28,12},{1,17},{... | collective-permute-start | bytes 1179656 | tf_op jit(solution)/shard_map/ppermute | solution.py:30
  155.5 15.2 %collective-permute-start.48 = (bf16[2,384,256]{2,1,0:T(8,128)(2,1)S(1)}, bf16[2,384,256]{2,1,0:T(8,128)(2,1)S(1)}, u32[]{:S(2)}, u32[]{:S(2)}) collective-permute-start(bf16[2,384,256]{2,1,0:T(8,128)(2,1)S(1)} %get-tuple-element.131), channel_id=1, source_target_pairs={{0,8},{4,12},{8,0},{12,4},{16,24},{20,28},{24,16},{28,20},{1,9},{5... | collective-permute-start | bytes 1179656 | tf_op jit(solution)/shard_map/ppermute | solution.py:30
  163.1 11.1 %collective-permute-start.45 = (bf16[1,384,256]{2,1,0:T(8,128)(2,1)}, bf16[1,384,256]{2,1,0:T(8,128)(2,1)S(1)}, u32[]{:S(2)}, u32[]{:S(2)}) collective-permute-start(bf16[1,384,256]{2,1,0:T(8,128)(2,1)} %get-tuple-element.128), channel_id=1, source_target_pairs={{0,16},{4,20},{8,24},{12,28},{16,0},{20,4},{24,8},{28,12},{1,17},{... | collective-permute-start | bytes 589832 | tf_op jit(solution)/shard_map/ppermute | solution.py:30
  164.4 9.7 %collective-permute-start.46 = (bf16[1,384,256]{2,1,0:T(8,128)(2,1)S(1)}, bf16[1,384,256]{2,1,0:T(8,128)(2,1)S(1)}, u32[]{:S(2)}, u32[]{:S(2)}) collective-permute-start(bf16[1,384,256]{2,1,0:T(8,128)(2,1)S(1)} %get-tuple-element.129), channel_id=1, source_target_pairs={{0,8},{4,12},{8,0},{12,4},{16,24},{20,28},{24,16},{28,20},{1,9},{5... | collective-permute-start | bytes 589832 | tf_op jit(solution)/shard_map/ppermute | solution.py:30
  (28 other events, 166.7 us)
